TPU v7x, 128 devices: a whole 4x4x4 slice. The times are simulated.
128 devices in a mesh: dp: 32 (over x, z, y_hi), seq: 4 (over y_lo, core).
Axes of the slice: x: 4, y: 4 (y_hi: 2, y_lo: 2; y = y_hi * 2 + y_lo), z: 4, core: 2. Of those that a mesh axis runs over, the one named last changes fastest.
Arguments:
- query_proj: bfloat16 [32768, 2560], P(('dp', 'seq')), may hold values from -80 to 80
- key_proj: bfloat16 [32768, 2560], P(('dp', 'seq')), may hold values from -4 to 4
- value_proj: bfloat16 [32768, 2560], P(('dp', 'seq')), may hold values from -5 to 5
- cotangent: bfloat16 [32768, 2560], P(('dp', 'seq')), may hold values from -48 to 48
- out_weight: bfloat16 [2560, 2560], P('seq'), may hold values from -0.125 to 0.125
- tile_list: int32 [8, 6], replicated, may hold values from 0 to 7, as said below
- owners: int32 [400, 1], replicated, may hold values from 0 to 31; in each aligned block of 100 rows (0 to 99, 100 to 199, ...) at most 7 rows name the same one
- master: float32 [32, 28, 128, 128], P('dp', 'seq'), may hold values from -0.3 to 0.3
- moment_one: float32 [32, 28, 128, 128], P('dp', 'seq'), may hold values from -24 to 24
- moment_two: float32 [32, 28, 128, 128], P('dp', 'seq'), may hold values from 10 to 1000
- average: float32 [32, 28, 128, 128], P('dp', 'seq'), may hold values from -0.3 to 0.3
Outputs:
- query_grad: bfloat16 [32768, 2560], P(('dp', 'seq'))
- key_grad: bfloat16 [32768, 2560], P(('dp', 'seq'))
- value_grad: bfloat16 [32768, 2560], P(('dp', 'seq'))
- new_weight: bfloat16 [2560, 2560], P('seq')
- new_master: float32 [32, 28, 128, 128], P('dp', 'seq')
- new_moment_one: float32 [32, 28, 128, 128], P('dp', 'seq')
- new_moment_two: float32 [32, 28, 128, 128], P('dp', 'seq')
- new_average: float32 [32, 28, 128, 128], P('dp', 'seq')
Inputs may be any that keep to these rules, and one draw needn't show every extreme that they name: `tile_list`: row i lists 6 different key tiles, the first being i itself. `owners`: among the 100 blocks of one group no data index owns more than 7, and in some group one owns exactly 7.
All inputs are finite; a program needn't handle non-finite values.
Results may differ from a plain program's by a relative error of at most 0.0085.
Values may be sent and summed in bfloat16 or wider, within the bound.
A program may use at most 320 MiB of HBM per device.

v0:
```python
import math

import jax
import jax.numpy as jnp
from jax import lax
from jax.sharding import PartitionSpec as P

learn_rate = 0.001
beta_one = 0.9
beta_two = 0.95
adam_eps = 1e-08
weight_decay = 0.1
ema_keep = 0.99
bias_one = 1.0 - (0.9**50) ** 2
bias_two = 1.0 - (0.95**50) ** 2


def attend_forward(query, keyed, valued, tile_list):
    length, head_count, head_width = query.shape
    tile_count, kcount = tile_list.shape
    tile_len = length // tile_count
    score_scale = 1.0 / math.sqrt(head_width)
    query_t = query.reshape(tile_count, tile_len, head_count, head_width)
    key_sel = keyed.reshape(tile_count, tile_len, head_count, head_width)[tile_list]
    key_sel = key_sel.reshape(tile_count, kcount * tile_len, head_count, head_width)
    value_sel = valued.reshape(tile_count, tile_len, head_count, head_width)[tile_list]
    value_sel = value_sel.reshape(tile_count, kcount * tile_len, head_count, head_width)
    scores = (
        jnp.einsum("iqhd,ikhd->ihqk", query_t, key_sel, preferred_element_type=jnp.float32)
        * score_scale
    )
    row_top = jnp.max(scores, axis=-1, keepdims=True)
    exp_scores = jnp.exp(scores - row_top)
    softmax_f = exp_scores / jnp.sum(exp_scores, axis=-1, keepdims=True)
    softmax_b = softmax_f.astype(jnp.bfloat16)
    attention = jnp.einsum(
        "ihqk,ikhd->iqhd", softmax_b, value_sel, preferred_element_type=jnp.float32
    )
    attention = attention.astype(jnp.bfloat16).reshape(length, head_count * head_width)
    return (attention, (query_t, key_sel, value_sel, softmax_f, softmax_b))


def attend_backward(saved_terms, d_attn, tile_list):
    query_t, key_sel, value_sel, softmax_f, softmax_b = saved_terms
    tile_count, tile_len, head_count, head_width = query_t.shape
    kcount = tile_list.shape[1]
    score_scale = 1.0 / math.sqrt(head_width)
    d_tiles = d_attn.reshape(tile_count, tile_len, head_count, head_width)
    d_prob = jnp.einsum("iqhd,ikhd->ihqk", d_tiles, value_sel, preferred_element_type=jnp.float32)
    row_delta = jnp.sum(softmax_f * d_prob, axis=-1, keepdims=True)
    d_score = (softmax_f * (d_prob - row_delta) * score_scale).astype(jnp.bfloat16)
    flat = (tile_count * tile_len, head_count * head_width)
    query_grad = jnp.einsum("ihqk,ikhd->iqhd", d_score, key_sel, preferred_element_type=jnp.float32)
    query_grad = query_grad.astype(jnp.bfloat16).reshape(flat)
    key_part = jnp.einsum("ihqk,iqhd->ikhd", d_score, query_t, preferred_element_type=jnp.float32)
    value_part = jnp.einsum(
        "ihqk,iqhd->ikhd", softmax_b, d_tiles, preferred_element_type=jnp.float32
    )
    key_part = key_part.reshape(tile_count, kcount, tile_len * head_count * head_width)
    value_part = value_part.reshape(tile_count, kcount, tile_len * head_count * head_width)
    tile_ids = jnp.arange(tile_count, dtype=jnp.int32)
    onehot = (tile_list[:, :, None] == tile_ids[None, None, :]).astype(jnp.float32)
    high = lax.Precision.HIGHEST
    key_grad = (
        jnp.einsum("ijn,ijc->nc", onehot, key_part, precision=high)
        .astype(jnp.bfloat16)
        .reshape(flat)
    )
    value_grad = (
        jnp.einsum("ijn,ijc->nc", onehot, value_part, precision=high)
        .astype(jnp.bfloat16)
        .reshape(flat)
    )
    return (query_grad, key_grad, value_grad)


def adam_step(master_in, first_in, second_in, mean_in, gradient):
    first_out = beta_one * first_in + (1.0 - beta_one) * gradient
    second_out = beta_two * second_in + (1.0 - beta_two) * gradient * gradient
    direction = first_out / bias_one / (jnp.sqrt(second_out / bias_two) + adam_eps)
    master_out = master_in - learn_rate * (direction + weight_decay * master_in)
    mean_out = ema_keep * mean_in + (1.0 - ema_keep) * master_out
    return (master_out, first_out, second_out, mean_out)


def local(
    query_proj,
    key_proj,
    value_proj,
    cotangent,
    out_weight,
    tile_list,
    owners,
    master,
    moment_one,
    moment_two,
    average,
):
    n_data = lax.axis_size("dp")
    head_width = master.shape[2]
    block_cols = master.shape[3]
    slot_count = master.shape[1]
    heads_here = out_weight.shape[0] // head_width
    seq_len = cotangent.shape[0] * lax.axis_size("seq")
    q_heads, k_heads, v_heads = (
        lax.all_to_all(query_proj, "seq", split_axis=1, concat_axis=0, tiled=True),
        lax.all_to_all(key_proj, "seq", split_axis=1, concat_axis=0, tiled=True),
        lax.all_to_all(value_proj, "seq", split_axis=1, concat_axis=0, tiled=True),
    )
    head_shape = (seq_len, heads_here, head_width)
    attention, saved_terms = attend_forward(
        q_heads.reshape(head_shape),
        k_heads.reshape(head_shape),
        v_heads.reshape(head_shape),
        tile_list,
    )
    piece_rows = lax.all_gather(cotangent, "seq", axis=0, tiled=True)
    grad_acc = lax.dot_general(
        attention, piece_rows, (((0,), (0,)), ((), ())), preferred_element_type=jnp.float32
    )
    d_rows = lax.dot_general(
        piece_rows, out_weight, (((1,), (1,)), ((), ())), preferred_element_type=jnp.float32
    )
    d_acc = d_rows.astype(jnp.bfloat16)
    query_grad, key_grad, value_grad = attend_backward(
        saved_terms, d_acc.reshape(head_shape), tile_list
    )
    q_back, k_back, v_back = (
        lax.all_to_all(query_grad, "seq", split_axis=0, concat_axis=1, tiled=True),
        lax.all_to_all(key_grad, "seq", split_axis=0, concat_axis=1, tiled=True),
        lax.all_to_all(value_grad, "seq", split_axis=0, concat_axis=1, tiled=True),
    )
    per_row = cotangent.shape[1] // block_cols
    blocks_here = heads_here * per_row
    block_grad = grad_acc.reshape(heads_here, head_width, per_row, block_cols).transpose(0, 2, 1, 3)
    block_grad = block_grad.reshape(blocks_here, head_width, block_cols)
    group_owner = lax.dynamic_slice_in_dim(
        owners[:, 0], lax.axis_index("seq") * blocks_here, blocks_here, 0
    )
    block_order = jnp.arange(blocks_here, dtype=jnp.int32)
    earlier = (group_owner[:, None] == group_owner[None, :]) & (
        block_order[None, :] < block_order[:, None]
    )
    slot_of = jnp.sum(earlier.astype(jnp.int32), axis=1)
    slot_place = group_owner * slot_count + slot_of
    slot_ids = jnp.arange(slot_count, dtype=jnp.int32)
    owned_match = (
        (group_owner[None, :] == lax.axis_index("dp")) & (slot_of[None, :] == slot_ids[:, None])
    ).astype(jnp.float32)
    filled = jnp.sum(owned_match, axis=1) > 0.5
    high = lax.Precision.HIGHEST
    summed = lax.psum(block_grad.astype(jnp.bfloat16), "dp").astype(jnp.float32) / n_data
    owned_grad = jnp.einsum("sb,bxc->sxc", owned_match, summed, precision=high)
    stepped = adam_step(master[0], moment_one[0], moment_two[0], average[0], owned_grad)
    keep = filled[:, None, None]
    new_master = jnp.where(keep, stepped[0], master[0])
    new_moment_one = jnp.where(keep, stepped[1], moment_one[0])
    new_moment_two = jnp.where(keep, stepped[2], moment_two[0])
    new_average = jnp.where(keep, stepped[3], average[0])
    fresh_bf = new_master.astype(jnp.bfloat16)
    gathered = lax.all_gather(fresh_bf[None], "dp", axis=0, tiled=True)
    blocks_new = gathered.reshape(n_data * slot_count, head_width, block_cols)[slot_place]
    new_weight = blocks_new.reshape(heads_here, per_row, head_width, block_cols).transpose(
        0, 2, 1, 3
    )
    new_weight = new_weight.reshape(heads_here * head_width, per_row * block_cols)
    return (
        q_back,
        k_back,
        v_back,
        new_weight,
        new_master[None],
        new_moment_one[None],
        new_moment_two[None],
        new_average[None],
    )


def solution(mesh):
    in_specs = (
        P(("dp", "seq"), None),
        P(("dp", "seq"), None),
        P(("dp", "seq"), None),
        P(("dp", "seq"), None),
        P("seq", None),
        P(),
        P(),
        P("dp", "seq", None, None),
        P("dp", "seq", None, None),
        P("dp", "seq", None, None),
        P("dp", "seq", None, None),
    )
    out_specs = (
        P(("dp", "seq"), None),
        P(("dp", "seq"), None),
        P(("dp", "seq"), None),
        P("seq", None),
        P("dp", "seq", None, None),
        P("dp", "seq", None, None),
        P("dp", "seq", None, None),
        P("dp", "seq", None, None),
    )
    return jax.shard_map(local, mesh=mesh, in_specs=in_specs, out_specs=out_specs, check_vma=False)
```

profile of v0, /device:TPU:0, one launch (start us, length us, event | category | flops | bytes accessed | tf_op | source)
XLA Modules:
  0.0 879.9 jit_solution(15398684533636585052)
XLA Ops:
  10.6 4.3 all-to-all-start.2
  17.3 21.7 %all-to-all-done.2 = bf16[256,4,640]{0,2,1:T(8,128)(2,1)} async-done(((bf16[256,4,640]{0,2,1:T(8,128)(2,1)}), bf16[256,4,640]{0,2,1:T(8,128)(2,1)}, u32[]{:S(2)}, u32[]{:S(2)}) %all-to-all-start.2) | async-done | bytes 1310752 | tf_op jit(solution)/shard_map/all_to_all | solution.py:108
  39.0 4.3 all-to-all-start
  45.7 29.3 %all-to-all-done = bf16[256,4,640]{0,2,1:T(8,128)(2,1)} async-done(((bf16[256,4,640]{0,2,1:T(8,128)(2,1)}), bf16[256,4,640]{0,2,1:T(8,128)(2,1)}, u32[]{:S(2)}, u32[]{:S(2)}) %all-to-all-start) | async-done | bytes 1310752 | tf_op jit(solution)/shard_map/all_to_all | solution.py:107
  75.0 4.3 all-to-all-start.1
  79.5 3.4 copy.230
  82.9 4.0 reshape_reshape.15
  86.9 2.7 copy.231
  89.6 6.9 gather_fusion.1
  96.5 9.8 %copy.232 = bf16[48,128,5,128]{3,1,0,2:T(8,128)(2,1)} copy(bf16[48,128,5,128]{3,1,2,0:T(8,128)(2,1)} %gather_fusion.1) | data formatting | bytes 15728640 | tf_op jit(solution)/shard_map/gather | solution.py:26
  106.3 3.4 copy.221
  109.7 3.5 reshape_reshape.12
  113.2 2.7 copy.222
  115.9 7.0 gather_fusion
  122.9 9.8 %copy.223 = bf16[48,128,5,128]{3,1,0,2:T(8,128)(2,1)} copy(bf16[48,128,5,128]{3,1,2,0:T(8,128)(2,1)} %gather_fusion) | data formatting | bytes 15728640 | tf_op jit(solution)/shard_map/gather | solution.py:24
  132.7 3.4 copy.225
  136.1 3.5 reshape_reshape.13
  139.5 2.9 copy.227
  142.4 11.2 %fusion.20 = f32[8,5,768,128]{3,2,1,0:T(8,128)} fusion(bf16[8,128,5,128]{3,1,2,0:T(8,128)(2,1)} %copy.227, bf16[8,768,5,128]{3,1,0,2:T(8,128)(2,1)} %bitcast.177), kind=kOutput, calls=%fused_computation.24 | convolution fusion | flops 1006632960 | bytes 24903680 | tf_op jit(solution)/shard_map/iqhd,ikhd->ihqk/dot_general | solution.py:29
  153.7 17.4 %fusion.88 = (f32[8,5,128]{2,1,0:T(8,128)S(1)}, f32[8,5,128,768]{2,3,1,0:T(8,128)}) fusion(f32[8,5,768,128]{3,2,1,0:T(8,128)} %fusion.20), kind=kOutput, calls=%fused_computation.93 | output fusion | flops 15729407 | bytes 31477760 | tf_op jit(solution)/shard_map/sub | solution.py:33
  171.1 20.2 %fusion.48 = bf16[8,128,5,128]{1,3,2,0:T(8,128)(2,1)} fusion(bf16[8,768,5,128]{3,1,0,2:T(8,128)(2,1)} %bitcast.175, f32[8,5,128]{2,1,0:T(8,128)S(1)} %get-tuple-element.62, f32[8,5,768,128]{3,2,1,0:T(8,128)} %fusion.20), kind=kOutput, calls=%fused_computation.43 | convolution fusion | flops 1026955008 | bytes 24924160 | tf_op jit(solution)/shard_map/ihqk,ikhd->iqhd/dot_general | solution.py:36
  194.9 7.9 copy.254
  202.9 6.2 convolution_convert_fusion
  209.0 3.8 copy.255
  214.0 365.7 %all-reduce.2.cloned.1.call-done = bf16[100,128,128]{2,0,1:T(8,128)(2,1)} async-done(((bf16[100,128,128]{2,0,1:T(8,128)(2,1)}), bf16[100,128,128]{2,0,1:T(8,128)(2,1)}) %all-reduce.2.cloned.1.call-update) | async-done | bytes 3276816 | tf_op jit(solution)/shard_map/psum | solution.py:152
  579.8 4.7 fusion.27
  584.4 2.9 fusion.55
  589.0 7.8 convolution_convert_fusion.1
  596.8 4.5 reshape.137
  601.3 3.4 copy.246
  604.7 11.0 %fusion.25 = f32[8,5,128,768]{2,3,1,0:T(8,128)} fusion(bf16[8,128,5,128]{1,3,2,0:T(8,128)(2,1)S(1)} %copy.246, bf16[8,768,5,128]{3,1,0,2:T(8,128)(2,1)} %bitcast.176), kind=kOutput, calls=%fused_computation.29 | convolution fusion | flops 1006632960 | bytes 24903680 | tf_op jit(solution)/shard_map/iqhd,ikhd->ihqk/dot_general | solution.py:49
  615.7 28.7 %fusion.43 = bf16[8,128,5,128]{1,3,2,0:T(8,128)(2,1)} fusion(f32[8,5,128,768]{2,3,1,0:T(8,128)} %fusion.25, bf16[8,768,5,128]{3,1,0,2:T(8,128)(2,1)} %bitcast.178, f32[8,5,128,768]{2,3,1,0:T(8,128)} %get-tuple-element.63, f32[8,5,128]{2,1,0:T(8,128)S(1)} %get-tuple-element.62), kind=kOutput, calls=%fused_computation.42 | convolution fusion | flops 1034819328 | bytes 40652800 | tf_op jit(solution)/shard_map/ihqk,ikhd->iqhd/dot_general | solution.py:53
  644.4 3.3 copy.239
  647.7 3.8 all_to_all.87
  654.1 4.3 all-to-all-start.3
  658.4 27.2 %convolution_bitcast_fusion.3 = f32[8,768,5,128]{3,1,2,0:T(8,128)} fusion(bf16[8,128,5,128]{3,1,2,0:T(8,128)(2,1)S(1)} %copy-done.2, f32[8,5,128,768]{2,3,1,0:T(8,128)} %fusion.25, f32[8,5,128,768]{2,3,1,0:T(8,128)} %get-tuple-element.63, f32[8,5,128]{2,1,0:T(8,128)S(1)} %get-tuple-element.62), kind=kOutput, calls=%fused_computation.20 | convolution fusion | flops 1034163968 | bytes 48517120 | tf_op jit(solution)/shard_map/ihqk,iqhd->ikhd/dot_general | solution.py:55
  685.6 20.5 %copy.243 = f32[8,768,5,128]{3,2,1,0:T(8,128)} copy(f32[8,768,5,128]{3,1,2,0:T(8,128)} %convolution_bitcast_fusion.3) | data formatting | bytes 31457280 | tf_op jit(solution)/shard_map/ihqk,iqhd->ikhd/transpose | solution.py:55
  706.1 18.2 %reshape.94 = f32[8,6,81920]{2,1,0:T(8,128)} reshape(f32[8,768,5,128]{3,2,1,0:T(8,128)} %copy.243) | data formatting | bytes 31457280 | tf_op jit(solution)/shard_map/reshape | solution.py:59
  724.3 24.0 %fusion.2 = bf16[8,81920]{1,0:T(8,128)(2,1)S(1)} fusion(f32[8,6,81920]{2,1,0:T(8,128)} %reshape.94, s32[8,6]{0,1:T(8,128)S(1)} %copy.241), kind=kOutput, calls=%fused_computation.7 | convolution fusion | flops 378143104 | bytes 17039552 | tf_op jit(solution)/shard_map/ijn,ijc->nc/dot_general | solution.py:65
  750.0 4.5 all-to-all-start.4
  754.5 18.6 %convolution_bitcast_fusion.2 = f32[8,768,5,128]{1,3,2,0:T(8,128)} fusion(bf16[8,128,5,128]{1,3,2,0:T(8,128)(2,1)S(1)} %copy.246, f32[8,5,128]{2,1,0:T(8,128)S(1)} %get-tuple-element.62, f32[8,5,768,128]{3,2,1,0:T(8,128)} %fusion.20), kind=kOutput, calls=%fused_computation.19 | convolution fusion | flops 1026299648 | bytes 32788480 | tf_op jit(solution)/shard_map/ihqk,iqhd->ikhd/dot_general | solution.py:56
  773.1 20.7 %copy.248 = f32[8,768,5,128]{3,2,1,0:T(8,128)} copy(f32[8,768,5,128]{1,3,2,0:T(8,128)} %convolution_bitcast_fusion.2) | data formatting | bytes 31457280 | tf_op jit(solution)/shard_map/ihqk,iqhd->ikhd/transpose | solution.py:56
  793.8 18.2 %reshape.95 = f32[8,6,81920]{2,1,0:T(8,128)} reshape(f32[8,768,5,128]{3,2,1,0:T(8,128)} %copy.248) | data formatting | bytes 31457280 | tf_op jit(solution)/shard_map/reshape | solution.py:60
  812.0 23.9 %fusion.3 = bf16[8,81920]{1,0:T(8,128)(2,1)S(1)} fusion(f32[8,6,81920]{2,1,0:T(8,128)} %reshape.95, s32[8,6]{0,1:T(8,128)S(1)} %copy.241), kind=kOutput, calls=%fused_computation.8 | convolution fusion | flops 378143104 | bytes 17039552 | tf_op jit(solution)/shard_map/ijn,ijc->nc/dot_general | solution.py:70
  837.6 3.8 all-to-all-start.5
  847.1 11.5 %all-to-all-done.5 = bf16[4,256,640]{2,1,0:T(8,128)(2,1)S(1)} async-done(((bf16[4,256,640]{2,1,0:T(8,128)(2,1)}), bf16[4,256,640]{2,1,0:T(8,128)(2,1)S(1)}, u32[]{:S(2)}, u32[]{:S(2)}) %all-to-all-start.5) | async-done | bytes 1310752 | tf_op jit(solution)/shard_map/all_to_all | solution.py:131
  860.7 6.0 gather_fusion.2
  866.7 4.1 copy.259
  (59 shorter events, 30.7 us)
Async XLA Ops:
  7.2 581.9 %copy-start = (bf16[640,2560]{1,0:T(8,128)(2,1)S(1)}, bf16[640,2560]{1,0:T(8,128)(2,1)}, u32[]{:S(2)}) copy-start(bf16[640,2560]{1,0:T(8,128)(2,1)} %param.15) | copy-start | bytes 9830404
  7.2 187.7 %all-gather.4.cloned.1.call-start = ((), (), s32[]{:S(2)}) async-start(), calls=%async_computation.6 | async-start | bytes 6553600 | tf_op jit(solution)/shard_map/all_gather | solution.py:117
  7.9 71.5 %copy-start.7 = (s32[8,6]{1,0:T(8,128)S(1)}, s32[8,6]{1,0:T(8,128)}, u32[]{:S(2)}) copy-start(s32[8,6]{1,0:T(8,128)} %param.16) | copy-start | bytes 580
  10.6 28.4 %all-to-all-start.2 = ((bf16[256,4,640]{0,2,1:T(8,128)(2,1)}), bf16[256,4,640]{0,2,1:T(8,128)(2,1)}, u32[]{:S(2)}, u32[]{:S(2)}) async-start(bf16[256,4,640]{0,2,1:T(8,128)(2,1)} %bitcast.186), calls=%async_computation.2 | async-start | bytes 2621440 | tf_op jit(solution)/shard_map/all_to_all | solution.py:108
  39.0 36.0 %all-to-all-start = ((bf16[256,4,640]{0,2,1:T(8,128)(2,1)}), bf16[256,4,640]{0,2,1:T(8,128)(2,1)}, u32[]{:S(2)}, u32[]{:S(2)}) async-start(bf16[256,4,640]{0,2,1:T(8,128)(2,1)} %bitcast.185), calls=%async_computation | async-start | bytes 2621440 | tf_op jit(solution)/shard_map/all_to_all | solution.py:107
  75.0 57.7 %all-to-all-start.1 = ((bf16[256,4,640]{0,2,1:T(8,128)(2,1)}), bf16[256,4,640]{0,2,1:T(8,128)(2,1)}, u32[]{:S(2)}, u32[]{:S(2)}) async-start(bf16[256,4,640]{0,2,1:T(8,128)(2,1)} %bitcast.183), calls=%async_computation.1 | async-start | bytes 2621440 | tf_op jit(solution)/shard_map/all_to_all | solution.py:106
  79.3 500.4 %all-reduce.2.cloned.1.call-start = ((), (), s32[]{:S(2)}) async-start(), calls=%async_computation.7 | async-start | bytes 6815744 | tf_op jit(solution)/shard_map/psum | solution.py:152
  212.9 647.8 %all-gather.6.cloned.1.call-start = ((), (), s32[]{:S(2)}) async-start(), calls=%async_computation.8 | async-start | bytes 7569408 | tf_op jit(solution)/shard_map/all_gather | solution.py:161
  213.9 383.0 %copy-start.10 = (s32[100]{0:T(128)}, s32[100]{0:T(128)S(1)}, u32[]{:S(2)}) copy-start(s32[100]{0:T(128)S(1)} %convert_reduce_fusion) | copy-start | bytes 1204
  214.0 374.9 %copy-start.8 = (pred[7]{0:T(512)(128)(4,1)}, pred[7]{0:T(512)(128)(4,1)S(1)}, u32[]{:S(2)}) copy-start(pred[7]{0:T(512)(128)(4,1)S(1)} %broadcast_compare_fusion) | copy-start | bytes 25
  579.8 8.4 copy-start.3
  587.3 0.8 copy-start.5
  644.4 14.0 %copy-start.2 = (bf16[8,128,5,128]{3,1,2,0:T(8,128)(2,1)S(1)}, bf16[8,128,5,128]{3,1,2,0:T(8,128)(2,1)}, u32[]{:S(2)}) copy-start(bf16[8,128,5,128]{3,1,2,0:T(8,128)(2,1)} %copy.227) | copy-start | bytes 3932164
  654.1 95.9 %all-to-all-start.3 = ((bf16[4,256,640]{1,2,0:T(8,128)(2,1)}), bf16[4,256,640]{1,2,0:T(8,128)(2,1)}, u32[]{:S(2)}, u32[]{:S(2)}) async-start(bf16[4,256,640]{1,2,0:T(8,128)(2,1)} %copy.240), calls=%async_computation.3 | async-start | bytes 2621440 | tf_op jit(solution)/shard_map/all_to_all | solution.py:129
  750.0 87.6 %all-to-all-start.4 = ((bf16[4,256,640]{2,1,0:T(8,128)(2,1)}), bf16[4,256,640]{2,1,0:T(8,128)(2,1)}, u32[]{:S(2)}, u32[]{:S(2)}) async-start(bf16[4,256,640]{2,1,0:T(8,128)(2,1)} %all_to_all.91), calls=%async_computation.4 | async-start | bytes 2621440 | tf_op jit(solution)/shard_map/all_to_all | solution.py:130
  812.0 29.4 %copy-start.11 = (s32[100]{0:T(128)S(1)}, s32[100]{0:T(128)}, u32[]{:S(2)}) copy-start(s32[100]{0:T(128)} %copy-done.10) | copy-start | bytes 1204
  835.9 23.9 %copy-start.4 = (f32[1,7,128,128]{3,2,1,0:T(8,128)S(1)}, f32[1,7,128,128]{3,2,1,0:T(8,128)}, u32[]{:S(2)}) copy-start(f32[1,7,128,128]{3,2,1,0:T(8,128)} %param.18) | copy-start | bytes 1376260
  835.9 23.9 %copy-start.6 = (f32[7,128,128]{2,1,0:T(8,128)S(1)}, f32[7,128,128]{2,1,0:T(8,128)}, u32[]{:S(2)}) copy-start(f32[7,128,128]{2,1,0:T(8,128)} %copy-done.5) | copy-start | bytes 1376260
  836.0 23.9 %copy-start.9 = (pred[7]{0:T(512)(128)(4,1)S(1)}, pred[7]{0:T(512)(128)(4,1)}, u32[]{:S(2)}) copy-start(pred[7]{0:T(512)(128)(4,1)} %copy-done.8) | copy-start | bytes 25
  837.6 21.0 %all-to-all-start.5 = ((bf16[4,256,640]{2,1,0:T(8,128)(2,1)}), bf16[4,256,640]{2,1,0:T(8,128)(2,1)S(1)}, u32[]{:S(2)}, u32[]{:S(2)}) async-start(bf16[4,256,640]{2,1,0:T(8,128)(2,1)} %all_to_all.95), calls=%async_computation.5 | async-start | bytes 2621440 | tf_op jit(solution)/shard_map/all_to_all | solution.py:131
  860.7 12.4 %copy-start.1 = (bf16[640,2560]{1,0:T(8,128)(2,1)S(1)}, bf16[640,2560]{1,0:T(8,128)(2,1)}, u32[]{:S(2)}) copy-start(bf16[640,2560]{1,0:T(8,128)(2,1)} %param.15) | copy-start | bytes 9830404
Sparse Core Ops, SparseCore 0:
  9.7 83.9 all-gather.3
  213.0 366.6 all-reduce.1
  589.1 112.7 all-gather.5
where the time goes:
time: 885 us; the launch traced here: 880 us
  waiting for transfers between devices  429 us (48%)
  local copies, waits for them, and re-layouts  204 us (23%)
  matrix products  184 us (21%)
  starting transfers between devices  25.6 us (3%)
  other arithmetic  23.9 us (3%)
  between operations  14.2 us (2%)
    psum x1, waiting for transfers between devices, local(): lax.psum(block_grad.astype(jnp.bfloat16), 'dp').astype(jnp.float32) / n_data  366 us
    all_to_all x1, waiting for transfers between devices, local(): lax.all_to_all(key_proj, 'seq', split_axis=1, concat_axis=0, tiled=True)  29.3 us
    dot_general x1, matrix products, attend_backward(): jnp.einsum('ihqk,ikhd->iqhd', d_score, key_sel, preferred_element_type=jn...  28.7 us
    dot_general x1, matrix products, attend_backward(): jnp.einsum('ihqk,iqhd->ikhd', d_score, query_t, preferred_element_type=jn...  27.2 us
    dot_general x1, matrix products, attend_backward(): jnp.einsum('ijn,ijc->nc', onehot, key_part, precision=high)  24 us
    dot_general x1, matrix products, attend_backward(): jnp.einsum('ijn,ijc->nc', onehot, value_part, precision=high)  23.9 us
    all_to_all x1, waiting for transfers between devices, local(): lax.all_to_all(value_proj, 'seq', split_axis=1, concat_axis=0, tiled=True)  21.7 us
    transpose x1, local copies, waits for them, and re-layouts, attend_backward(): jnp.einsum('ihqk,iqhd->ikhd', softmax_b, d_tiles, preferred_element_type=...  20.7 us
  transfers between devices with their start and end apart: 9, of which 4 were waited for; matrix products, arithmetic and copies ran while one was open for 41% of the time, Pallas kernels for 0%

commit v1 on v0

v1 whole, which is shorter than its diff:
```python
import math

import jax
import jax.numpy as jnp
from jax import lax
from jax.experimental import pallas as pl
from jax.experimental.pallas import tpu as pltpu
from jax.sharding import PartitionSpec as P

MESH = pl.DeviceIdType.MESH
BF = jnp.bfloat16
F32 = jnp.float32

learn_rate = 0.001
beta_one = 0.9
beta_two = 0.95
adam_eps = 1e-08
weight_decay = 0.1
ema_keep = 0.99
bias_one = 1.0 - (0.9**50) ** 2
bias_two = 1.0 - (0.95**50) ** 2

HD = 5
TOK = 256
LEN = 1024
OUTW = 2560
SL = 7
NEG = -1e30
SCALE = 1.0 / math.sqrt(128.0)
SCALE2 = SCALE * math.log2(math.e)
CC = 4


def aligned(value, step):
    return pl.multiple_of(value * step, step)


def remote(src, dst, send, recv, device):
    return pltpu.make_async_remote_copy(
        src_ref=src, dst_ref=dst, send_sem=send, recv_sem=recv, device_id=device, device_id_type=MESH
    )


def dot(a, b):
    return lax.dot_general(a, b, (((1,), (0,)), ((), ())), preferred_element_type=F32)


def dot_nt(a, b):
    return lax.dot_general(a, b, (((1,), (1,)), ((), ())), preferred_element_type=F32)


def place_of():
    dp = lax.axis_index("dp")
    return dp, lax.axis_index("seq"), dp // 8, (dp // 2) % 4, dp % 2


def dp_index(x, z, yh):
    return (x * 4 + z) * 2 + yh


def ring(value, step):
    return lax.rem(value + step, 4)


def attend_kernel(
    q_in, k_in, v_in, cot_in, w_in, bias,
    dq_out, dk_out, dv_out, rs_out,
    qkv, cot, w, da, back, kt, vt, att, dk_acc, dv_acc,
    gx, gz, r1x, r1z, s2x, s2z, r2x, r2z, s3, k3, r3,
    local_sem, back_local, cot_send, cot_recv, in_send, in_recv, back_send, back_recv,
    x1_send, x1_recv, z1_send, z1_recv, x2_send, x2_recv, z2_send, z2_recv, y_send, y_recv,
):
    dp, me, x, z, yh = place_of()
    sibling = me + 1 - 2 * lax.rem(me, 2)
    across = ring(me, 2)
    corner = ring(sibling, 2)
    peers = [ring(me, p) for p in (1, 2, 3)]
    sources = [ring(me, 4 - p) for p in (1, 2, 3)]
    inputs = (q_in, k_in, v_in)
    outputs = (dq_out, dk_out, dv_out)

    barrier = pltpu.get_barrier_semaphore()
    for t in peers:
        pl.semaphore_signal(barrier, inc=1, device_id=(dp, t), device_id_type=MESH)
    for p in (1, 2, 3):
        pl.semaphore_signal(barrier, inc=1, device_id=(dp_index(ring(x, p), z, yh), me), device_id_type=MESH)
        pl.semaphore_signal(barrier, inc=1, device_id=(dp_index(x, ring(z, p), yh), me), device_id_type=MESH)
    pl.semaphore_signal(barrier, inc=1, device_id=(dp_index(x, z, 1 - yh), me), device_id_type=MESH)
    pl.semaphore_wait(barrier, 10)

    def rows(s, n=TOK):
        return pl.ds(aligned(s, TOK), n)

    def cot_rows(s, c):
        return pl.ds(pl.multiple_of(s * TOK + c * (TOK // CC), TOK // CC), TOK // CC)

    def cot_cross(c):
        return remote(
            cot_in.at[pl.ds(c * (TOK // CC), TOK // CC)], cot.at[cot_rows(me, c)],
            cot_send.at[c], cot_recv.at[c], (dp, across),
        )

    def cot_sibling():
        return remote(cot_in, cot.at[rows(me)], cot_send.at[CC], cot_recv.at[CC], (dp, sibling))

    def cot_forward(c):
        part = cot.at[cot_rows(across, c)]
        return remote(part, part, cot_send.at[CC + 1 + c], cot_recv.at[CC + 1 + c], (dp, sibling))

    def cot_own():
        return pltpu.make_async_copy(cot_in, cot.at[rows(me)], local_sem.at[0])

    def w_own():
        return pltpu.make_async_copy(w_in, w, local_sem.at[1])

    def head_columns(t, h):
        return pl.ds(pl.multiple_of((t * HD + h) * 128, 128), 128)

    def head_send(h, a, p):
        t = peers[p]
        return remote(
            inputs[a].at[:, head_columns(t, h)], qkv.at[a, h, rows(me)],
            in_send.at[h, a, p], in_recv.at[h, a, p], (dp, t),
        )

    def head_recv(h, a, p):
        part = qkv.at[a, h, rows(sources[p])]
        return remote(part, part, in_send.at[h, a, p], in_recv.at[h, a, p], (dp, sources[p]))

    def head_own(h, a):
        return pltpu.make_async_copy(
            inputs[a].at[:, head_columns(me, h)], qkv.at[a, h, rows(me)], local_sem.at[2 + 3 * h + a]
        )

    def back_copy(h, a, p):
        t = peers[p]
        return remote(
            back.at[a, h, rows(t)], outputs[a].at[:, head_columns(me, h)],
            back_send.at[h, a, p], back_recv.at[h, a, p], (dp, t),
        )

    def back_recv_copy(h, a, p):
        return remote(
            back.at[a, h, rows(sources[p])], outputs[a].at[:, head_columns(sources[p], h)],
            back_send.at[h, a, p], back_recv.at[h, a, p], (dp, sources[p]),
        )

    def back_own(h, a):
        return pltpu.make_async_copy(
            back.at[a, h, rows(me)], outputs[a].at[:, head_columns(me, h)], back_local.at[h, a]
        )

    cot_own().start()
    w_own().start()
    for c in range(CC):
        cot_cross(c).start()
    cot_sibling().start()

    @pl.loop(0, HD)
    def _(h):
        for a in range(3):
            head_own(h, a).start()
            for p in range(3):
                head_send(h, a, p).start()

    for c in range(CC):
        cot_cross(c).wait_recv()
        cot_forward(c).start()
    cot_own().wait()
    w_own().wait()
    cot_sibling().wait_recv()
    for c in range(CC):
        cot_forward(c).wait_recv()

    @pl.loop(0, 4)
    def _(b):
        d_rows = dot_nt(cot[pl.ds(aligned(b, 256), 256), :], w[...]).astype(BF)
        for h in range(HD):
            da[h, pl.ds(aligned(b, 256), 256), :] = d_rows[:, h * 128 : (h + 1) * 128]

    def compute(h):
        kt[...] = qkv[1, h].T
        vt[...] = qkv[2, h].T
        dk_acc[...] = jnp.zeros_like(dk_acc)
        dv_acc[...] = jnp.zeros_like(dv_acc)

        @pl.loop(0, 4)
        def _(b):
            part = pl.ds(aligned(b, 256), 256)
            q_b = qkv[0, h, part, :]
            da_b = da[h, part, :]
            score = dot_nt(qkv[1, h], q_b).reshape(8, 128, 256) * SCALE2 + bias[b][:, None, :]
            score = score.reshape(LEN, 256)
            top = jnp.max(score, axis=0, keepdims=True)
            weight = jnp.exp2(score - top)
            total = jnp.sum(weight, axis=0, keepdims=True)
            prob = weight * (1.0 / total)
            prob_b = prob.astype(BF)
            d_prob = dot_nt(qkv[2, h], da_b)
            delta = jnp.sum(prob * d_prob, axis=0, keepdims=True)
            d_score = (prob * (d_prob - delta) * SCALE).astype(BF)
            att[:, part] = dot(vt[...], prob_b).astype(BF)
            back[0, h, part, :] = dot(kt[...], d_score).T.astype(BF)
            dk_acc[...] += dot(d_score, q_b)
            dv_acc[...] += dot(prob_b, da_b)

        back[1, h] = dk_acc[...].astype(BF)
        back[2, h] = dv_acc[...].astype(BF)

        @pl.loop(0, 4)
        def _(c):
            columns = pl.ds(aligned(c, 640), 640)
            grad = dot(att[...], cot[:, columns]).astype(BF)
            for xx in range(4):
                gx[h, xx, :, columns] = grad[xx * 32 : xx * 32 + 16]
                gz[h, c, xx] = grad[xx * 32 + 16 : xx * 32 + 32]

    def first_x(h, p):
        t = ring(x, p + 1)
        return remote(gx.at[h, t], r1x.at[h, p], x1_send.at[h, p], x1_recv.at[h, p], (dp_index(t, z, yh), me))

    def first_z(h, p):
        t = ring(z, p + 1)
        return remote(gz.at[h, t], r1z.at[h, p], z1_send.at[h, p], z1_recv.at[h, p], (dp_index(x, t, yh), me))

    def second_z(h, p):
        t = ring(z, p + 1)
        return remote(s2x.at[h, t], r2x.at[h, p], x2_send.at[h, p], x2_recv.at[h, p], (dp_index(x, t, yh), me))

    def second_x(h, p):
        t = ring(x, p + 1)
        return remote(s2z.at[h, t], r2z.at[h, p], z2_send.at[h, p], z2_recv.at[h, p], (dp_index(t, z, yh), me))

    def third(h):
        return remote(s3.at[h], r3.at[h], y_send.at[h], y_recv.at[h], (dp_index(x, z, 1 - yh), me))

    def after_first(h):
        for p in range(3):
            first_x(h, p).wait_recv()
            first_z(h, p).wait_recv()
        for c in range(4):
            columns = slice(c * 640, (c + 1) * 640)
            total = gx[h, x, :, columns].astype(F32)
            for p in range(3):
                total = total + r1x[h, p, :, columns].astype(F32)
            s2x[h, c] = total.astype(BF)
            total = gz[h, z, c].astype(F32)
            for p in range(3):
                total = total + r1z[h, p, c].astype(F32)
            s2z[h, c] = total.astype(BF)
        for p in range(3):
            second_z(h, p).start()
            second_x(h, p).start()

    def after_second(h):
        for p in range(3):
            second_z(h, p).wait_recv()
            second_x(h, p).wait_recv()
        even = s2x[h, z].astype(F32)
        odd = s2z[h, x].astype(F32)
        for p in range(3):
            even = even + r2x[h, p].astype(F32)
            odd = odd + r2z[h, p].astype(F32)
        first = jnp.full(even.shape, yh, jnp.int32) == 0
        k3[h] = jnp.where(first, even, odd)
        s3[h] = jnp.where(first, odd, even).astype(BF)
        third(h).start()

    @pl.loop(0, HD + 2)
    def _(h):
        @pl.when(h < HD)
        def _():
            for a in range(3):
                head_own(h, a).wait()
                for p in range(3):
                    head_recv(h, a, p).wait_recv()
            compute(h)
            for p in range(3):
                first_x(h, p).start()
                first_z(h, p).start()
            for a in range(3):
                back_own(h, a).start()
                for p in range(3):
                    back_copy(h, a, p).start()

        @pl.when((h >= 1) & (h <= HD))
        def _():
            after_first(h - 1)

        @pl.when(h >= 2)
        def _():
            after_second(h - 2)

    @pl.loop(0, HD)
    def _(h):
        third(h).wait_recv()
        total = (k3[h] + r3[h].astype(F32)).astype(BF)
        for c in range(5):
            rs_out[h * 5 + c] = total[:, c * 128 : (c + 1) * 128]

    for c in range(CC):
        cot_cross(c).wait_send()
        cot_forward(c).wait_send()
    cot_sibling().wait_send()

    @pl.loop(0, HD)
    def _(h):
        for p in range(3):
            first_x(h, p).wait_send()
            first_z(h, p).wait_send()
            second_x(h, p).wait_send()
            second_z(h, p).wait_send()
        third(h).wait_send()
        for a in range(3):
            back_own(h, a).wait()
            for p in range(3):
                head_send(h, a, p).wait_send()
                back_copy(h, a, p).wait_send()
                back_recv_copy(h, a, p).wait_recv()


def attend(q, k, v, cot, w, bias):
    any_space = pl.BlockSpec(memory_space=pl.ANY)
    vmem = pl.BlockSpec(memory_space=pltpu.VMEM)
    sems = lambda *shape: pltpu.SemaphoreType.DMA(shape)
    return pl.pallas_call(
        attend_kernel,
        out_shape=[jax.ShapeDtypeStruct((TOK, OUTW), BF)] * 3 + [jax.ShapeDtypeStruct((25, 16, 128), BF)],
        in_specs=[any_space] * 5 + [vmem],
        out_specs=[any_space] * 3 + [vmem],
        scratch_shapes=[
            pltpu.VMEM((3, HD, LEN, 128), BF),
            pltpu.VMEM((LEN, OUTW), BF),
            pltpu.VMEM((HD * 128, OUTW), BF),
            pltpu.VMEM((HD, LEN, 128), BF),
            pltpu.VMEM((3, HD, LEN, 128), BF),
            pltpu.VMEM((128, LEN), BF),
            pltpu.VMEM((128, LEN), BF),
            pltpu.VMEM((128, LEN), BF),
            pltpu.VMEM((LEN, 128), F32),
            pltpu.VMEM((LEN, 128), F32),
            pltpu.VMEM((HD, 4, 16, OUTW), BF),
            pltpu.VMEM((HD, 4, 4, 16, 640), BF),
            pltpu.VMEM((HD, 3, 16, OUTW), BF),
            pltpu.VMEM((HD, 3, 4, 16, 640), BF),
            pltpu.VMEM((HD, 4, 16, 640), BF),
            pltpu.VMEM((HD, 4, 16, 640), BF),
            pltpu.VMEM((HD, 3, 16, 640), BF),
            pltpu.VMEM((HD, 3, 16, 640), BF),
            pltpu.VMEM((HD, 16, 640), BF),
            pltpu.VMEM((HD, 16, 640), F32),
            pltpu.VMEM((HD, 16, 640), BF),
            sems(2 + 3 * HD),
            sems(HD, 3),
            sems(2 * CC + 1),
            sems(2 * CC + 1),
            *([sems(HD, 3, 3)] * 4),
            *([sems(HD, 3)] * 8),
            sems(HD),
            sems(HD),
        ],
        compiler_params=pltpu.CompilerParams(
            collective_id=0, has_side_effects=True, vmem_limit_bytes=56 * 1024 * 1024
        ),
    )(q, k, v, cot, w, bias)


def adam_step(master_in, first_in, second_in, mean_in, gradient):
    first_out = beta_one * first_in + (1.0 - beta_one) * gradient
    second_out = beta_two * second_in + (1.0 - beta_two) * gradient * gradient
    direction = first_out / bias_one / (jnp.sqrt(second_out / bias_two) + adam_eps)
    master_out = master_in - learn_rate * (direction + weight_decay * master_in)
    mean_out = ema_keep * mean_in + (1.0 - ema_keep) * master_out
    return (master_out, first_out, second_out, mean_out)


def update_kernel(
    rs, slot_from, filled, block_from, master, one, two, mean,
    w_out, master_out, one_out, two_out, mean_out,
    g_all, tx, rx, nb, t_all, nw,
    own_sem, g_send, g_recv, t_send, t_recv, n_send, n_recv, a_send, a_recv, w_send, w_recv,
):
    dp, me, x, z, yh = place_of()
    r = 2 * x + yh

    def member(k):
        j = lax.rem(r + k, 8)
        return j, dp_index(j // 2, z, lax.rem(j, 2))

    def z_peer(p):
        return dp_index(x, ring(z, p + 1), yh)

    barrier = pltpu.get_barrier_semaphore()
    for p in range(3):
        pl.semaphore_signal(barrier, inc=1, device_id=(z_peer(p), me), device_id_type=MESH)
    for k in range(1, 8):
        pl.semaphore_signal(barrier, inc=1, device_id=(member(k)[1], me), device_id_type=MESH)
    pl.semaphore_wait(barrier, 10)

    g_all[z] = rs[...]

    def gather_g(p):
        return remote(rs, g_all.at[z], g_send.at[p], g_recv.at[p], (z_peer(p), me))

    for p in range(3):
        gather_g(p).start()
    for p in range(3):
        gather_g(p).wait_recv()

    def to_owner(k):
        j, device = member(k)
        return remote(tx.at[j], rx.at[r], t_send.at[k - 1], t_recv.at[k - 1], (device, me))

    for k in range(1, 8):
        j, device = member(k)
        for s in range(SL):
            source = slot_from[device * SL + s]
            tx[j, s] = g_all[source // 25, lax.rem(source, 25)]
        to_owner(k).start()
    for s in range(SL):
        source = slot_from[dp * SL + s]
        rx[r, s] = g_all[source // 25, lax.rem(source, 25)]
    for k in range(1, 8):
        to_owner(k).wait_recv()

    for s in range(SL):
        gradient = rx[:, s].astype(F32).reshape(128, 128) * (1.0 / 32.0)
        before = (master[s], one[s], two[s], mean[s])
        stepped = adam_step(*before, gradient)
        keep = jnp.full((128, 128), filled[dp], jnp.int32) > s
        after = [jnp.where(keep, new, old) for new, old in zip(stepped, before)]
        master_out[s], one_out[s], two_out[s], mean_out[s] = after
        nb[:, s] = after[0].astype(BF).reshape(8, 16, 128)

    def from_owner(k):
        j, device = member(k)
        return remote(nb.at[j], t_all.at[z, r], n_send.at[k - 1], n_recv.at[k - 1], (device, me))

    for k in range(1, 8):
        from_owner(k).start()
    t_all[z, r] = nb[r]
    for k in range(1, 8):
        from_owner(k).wait_recv()

    def gather_t(p):
        return remote(t_all.at[z], t_all.at[z], a_send.at[p], a_recv.at[p], (z_peer(p), me))

    for p in range(3):
        gather_t(p).start()
    for p in range(3):
        gather_t(p).wait_recv()

    for h in range(HD):
        for c in range(20):
            source = block_from[h * 20 + c]
            nw[h, :, c * 128 : (c + 1) * 128] = t_all[source // 56, lax.rem(source // 7, 8), lax.rem(source, 7)]

    def gather_w(k):
        return remote(nw, w_out.at[:, r], w_send.at[k - 1], w_recv.at[k - 1], (member(k)[1], me))

    own = pltpu.make_async_copy(nw, w_out.at[:, r], own_sem)
    for k in range(1, 8):
        gather_w(k).start()
    own.start()
    for k in range(1, 8):
        gather_w(k).wait_recv()
    own.wait()
    for p in range(3):
        gather_g(p).wait_send()
        gather_t(p).wait_send()
    for k in range(1, 8):
        to_owner(k).wait_send()
        from_owner(k).wait_send()
        gather_w(k).wait_send()


def update(rs, slot_from, filled, block_from, master, one, two, mean):
    any_space = pl.BlockSpec(memory_space=pl.ANY)
    vmem = pl.BlockSpec(memory_space=pltpu.VMEM)
    smem = pl.BlockSpec(memory_space=pltpu.SMEM)
    sems = lambda *shape: pltpu.SemaphoreType.DMA(shape)
    return pl.pallas_call(
        update_kernel,
        out_shape=[jax.ShapeDtypeStruct((HD, 8, 16, OUTW), BF)] + [jax.ShapeDtypeStruct((SL, 128, 128), F32)] * 4,
        in_specs=[vmem, smem, smem, smem] + [vmem] * 4,
        out_specs=[any_space] + [vmem] * 4,
        scratch_shapes=[
            pltpu.VMEM((4, 25, 16, 128), BF),
            pltpu.VMEM((8, SL, 16, 128), BF),
            pltpu.VMEM((8, SL, 16, 128), BF),
            pltpu.VMEM((8, SL, 16, 128), BF),
            pltpu.VMEM((4, 8, SL, 16, 128), BF),
            pltpu.VMEM((HD, 16, OUTW), BF),
            pltpu.SemaphoreType.DMA,
            sems(3), sems(3), sems(7), sems(7), sems(7), sems(7), sems(3), sems(3), sems(7), sems(7),
        ],
        compiler_params=pltpu.CompilerParams(
            collective_id=1, has_side_effects=True, vmem_limit_bytes=32 * 1024 * 1024
        ),
    )(rs, slot_from, filled, block_from, master, one, two, mean)


def local(q, k, v, cot, w, tile_list, owners, master, one, two, mean):
    listed = jnp.any(tile_list[:, :, None] == jnp.arange(8, dtype=jnp.int32), axis=1)
    bias = jnp.where(listed, 0.0, NEG).astype(F32).reshape(4, 2, 8).transpose(0, 2, 1)
    bias = jnp.broadcast_to(bias[:, :, :, None], (4, 8, 2, 128)).reshape(4, 8, 256)

    group = lax.dynamic_slice_in_dim(owners[:, 0], lax.axis_index("seq") * 100, 100, 0)
    order = jnp.arange(100, dtype=jnp.int32)
    earlier = (group[:, None] == group[None, :]) & (order[None, :] < order[:, None])
    slot_of = jnp.sum(earlier.astype(jnp.int32), axis=1)
    data = jnp.arange(32, dtype=jnp.int32)
    slots = jnp.arange(SL, dtype=jnp.int32)
    filled = jnp.sum((group[None, :] == data[:, None]).astype(jnp.int32), axis=1)
    head, column = order // 20, order % 20
    lies_at = (column // 5) * 25 + head * 5 + column % 5
    match = (group[None, None, :] == data[:, None, None]) & (slot_of[None, None, :] == slots[None, :, None])
    slot_from = jnp.sum(jnp.where(match, lies_at[None, None, :], 0), axis=2).reshape(-1)
    plane = (group // 2) % 4
    block_from = (plane * 8 + (group // 8) * 2 + group % 2) * SL + slot_of

    dq, dk, dv, rs = attend(q, k, v, cot, w, bias)
    new_w, *state = update(rs, slot_from, filled, block_from, master[0], one[0], two[0], mean[0])
    return (dq, dk, dv, new_w.reshape(HD * 128, OUTW), *[s[None] for s in state])


def solution(mesh):
    tokens = P(("dp", "seq"), None)
    state = P("dp", "seq", None, None)
    return jax.shard_map(
        local,
        mesh=mesh,
        in_specs=(tokens,) * 4 + (P("seq", None), P(), P()) + (state,) * 4,
        out_specs=(tokens,) * 3 + (P("seq", None),) + (state,) * 4,
        check_vma=False,
    )
```

time: 885 us -> 224 us (0.25)
  the two profiles are of different devices: /device:TPU:0 before, /device:TPU:52 now
where the time goes in v1:
time: 224 us; the launch traced here: 223 us
  Pallas kernels  209 us (93%)
  local copies, waits for them, and re-layouts  12.7 us (6%)
    pallas_call x1, Pallas kernels, attend(): pl.pallas_call(attend_kernel, out_shape=[jax.ShapeDtypeStruct((TOK, OUTW)...  124 us
    pallas_call x1, Pallas kernels, update(): pl.pallas_call(update_kernel, out_shape=[jax.ShapeDtypeStruct((HD, 8, 16,...  84.7 us
    unnamed x25, local copies, waits for them, and re-layouts  11.1 us

profile of v1, /device:TPU:52, one launch (start us, length us, event | category | flops | bytes accessed | tf_op | source)
XLA Modules:
  0.0 223.5 jit_solution(12665882051203734426)
XLA Ops:
  0.6 0.8 dynamic-slice_bitcast_fusion
  1.4 0.2 convert_reduce_fusion
  1.6 0.8 multiply_add_fusion.block_from
  2.4 0.1 convert_reduce_fusion.1.filled
  2.5 0.2 select_reduce_fusion
  2.7 0.8 copy.19
  3.5 0.1 fusion.1
  3.6 0.1 copy.20
  3.7 0.1 reshape.120.slot_from
  3.8 0.7 broadcast_bitcast_fusion.bias
  4.5 0.0 copy-start
  4.5 0.0 copy-start.1
  4.5 0.0 copy-start.2
  4.5 0.0 copy-start.3
  4.5 123.9 %shard_map.170 = (bf16[256,2560]{1,0:T(8,128)(2,1)}, bf16[256,2560]{1,0:T(8,128)(2,1)}, bf16[256,2560]{1,0:T(8,128)(2,1)}, bf16[25,16,128]{2,1,0:T(8,128)(2,1)}) custom-call(bf16[256,2560]{1,0:T(8,128)(2,1)} %q_in.1, bf16[256,2560]{1,0:T(8,128)(2,1)} %k_in.1, bf16[256,2560]{1,0:T(8,128)(2,1)} %v_in.1, bf16[256,2560]{1,0:T(8,128)(2,1)} %cot_in.1, ...), custom_call_target="tpu_custom_call" | custom-call | tf_op jit(solution)/shard_map/pallas_call | solution.py:326
  128.4 0.0 copy-done
  128.4 0.0 copy-done.1
  128.4 0.0 copy-done.2
  128.4 0.0 copy-done.3
  128.4 0.0 copy-start.4
  128.4 0.9 copy-done.4
  129.3 0.0 copy-start.7
  129.3 84.7 %shard_map.171 = (bf16[5,8,16,2560]{3,2,1,0:T(8,128)(2,1)S(1)}, f32[7,128,128]{2,1,0:T(8,128)S(1)}, f32[7,128,128]{2,1,0:T(8,128)S(1)}, f32[7,128,128]{2,1,0:T(8,128)S(1)}, f32[7,128,128]{2,1,0:T(8,128)S(1)}) custom-call(bf16[25,16,128]{2,1,0:T(8,128)(2,1)S(1)} %copy-done.4, s32[224]{0:T(256)S(1)} %reshape.120.slot_from, s32[32]{0:T(128)S(1)} %convert_reduce_fusion.1.filled, ...), custom_call_target="tpu_custom_call" | custom-call | tf_op jit(solution)/shard_map/pallas_call | solution.py:482
  214.1 0.0 copy-done.7
  214.1 0.0 copy-start.6
  214.1 1.1 copy.29
  215.1 0.7 copy-done.6
  215.9 0.0 copy-start.5
  215.9 1.1 copy.30
  216.9 0.7 copy-done.5
  217.6 1.1 copy.31
  218.7 1.7 copy.32
  220.4 0.8 copy.33
  221.2 0.8 copy.34
  221.9 0.8 copy.35
  222.7 0.8 copy.36
  (4 shorter events, 0.0 us)
Async XLA Ops:
  4.5 123.9 %copy-start = (f32[1,7,128,128]{3,2,1,0:T(8,128)S(1)}, f32[1,7,128,128]{3,2,1,0:T(8,128)}, u32[]{:S(2)}) copy-start(f32[1,7,128,128]{3,2,1,0:T(8,128)} %param.18) | copy-start | bytes 1376260
  4.5 123.9 %copy-start.1 = (f32[1,7,128,128]{3,2,1,0:T(8,128)S(1)}, f32[1,7,128,128]{3,2,1,0:T(8,128)}, u32[]{:S(2)}) copy-start(f32[1,7,128,128]{3,2,1,0:T(8,128)} %param.19) | copy-start | bytes 1376260
  4.5 123.9 %copy-start.2 = (f32[1,7,128,128]{3,2,1,0:T(8,128)S(1)}, f32[1,7,128,128]{3,2,1,0:T(8,128)}, u32[]{:S(2)}) copy-start(f32[1,7,128,128]{3,2,1,0:T(8,128)} %param.20) | copy-start | bytes 1376260
  4.5 123.9 %copy-start.3 = (f32[1,7,128,128]{3,2,1,0:T(8,128)S(1)}, f32[1,7,128,128]{3,2,1,0:T(8,128)}, u32[]{:S(2)}) copy-start(f32[1,7,128,128]{3,2,1,0:T(8,128)} %param.21) | copy-start | bytes 1376260
  128.4 0.9 copy-start.4
  129.3 84.7 %copy-start.7 = (bf16[256,2560]{1,0:T(8,128)(2,1)S(1)}, bf16[256,2560]{1,0:T(8,128)(2,1)}, u32[]{:S(2)}) copy-start(bf16[256,2560]{1,0:T(8,128)(2,1)} %get-tuple-element.34) | copy-start | bytes 3932164
  214.1 1.8 copy-start.6
  215.9 1.8 copy-start.5

commit v2 on v1

--- a/solution.py
+++ b/solution.py
@@ -62,14 +62,30 @@
     return lax.rem(value + step, 4)
 
 
-def attend_kernel(
-    q_in, k_in, v_in, cot_in, w_in, bias,
-    dq_out, dk_out, dv_out, rs_out,
+def adam_step(master_in, first_in, second_in, mean_in, gradient):
+    first_out = beta_one * first_in + (1.0 - beta_one) * gradient
+    second_out = beta_two * second_in + (1.0 - beta_two) * gradient * gradient
+    direction = first_out / bias_one / (jnp.sqrt(second_out / bias_two) + adam_eps)
+    master_out = master_in - learn_rate * (direction + weight_decay * master_in)
+    mean_out = ema_keep * mean_in + (1.0 - ema_keep) * master_out
+    return (master_out, first_out, second_out, mean_out)
+
+
+def step_kernel(
+    q_in, k_in, v_in, cot_in, w_in, bias, slot_from, filled, block_from, *refs,
+):
+    states_in, refs = refs[:4], refs[4:]
+    dq_out, dk_out, dv_out, w_out = refs[:4]
+    states_out, refs = refs[4:8], refs[8:]
+    (
     qkv, cot, w, da, back, kt, vt, att, dk_acc, dv_acc,
     gx, gz, r1x, r1z, s2x, s2z, r2x, r2z, s3, k3, r3,
     local_sem, back_local, cot_send, cot_recv, in_send, in_recv, back_send, back_recv,
     x1_send, x1_recv, z1_send, z1_recv, x2_send, x2_recv, z2_send, z2_recv, y_send, y_recv,
-):
+    state, g_all, tx, rx, pieces, landed, w16,
+    state_sem, state_out_sem, g_send, g_recv, t_send, t_recv, n_send, n_recv,
+    a_send, a_recv, b_send, b_recv,
+    ) = refs
     dp, me, x, z, yh = place_of()
     sibling = me + 1 - 2 * lax.rem(me, 2)
     across = ring(me, 2)
@@ -82,11 +98,9 @@
     barrier = pltpu.get_barrier_semaphore()
     for t in peers:
         pl.semaphore_signal(barrier, inc=1, device_id=(dp, t), device_id_type=MESH)
-    for p in (1, 2, 3):
-        pl.semaphore_signal(barrier, inc=1, device_id=(dp_index(ring(x, p), z, yh), me), device_id_type=MESH)
-        pl.semaphore_signal(barrier, inc=1, device_id=(dp_index(x, ring(z, p), yh), me), device_id_type=MESH)
-    pl.semaphore_signal(barrier, inc=1, device_id=(dp_index(x, z, 1 - yh), me), device_id_type=MESH)
-    pl.semaphore_wait(barrier, 10)
+    for k in range(1, 32):
+        pl.semaphore_signal(barrier, inc=1, device_id=(lax.rem(dp + k, 32), me), device_id_type=MESH)
+    pl.semaphore_wait(barrier, 34)
 
     def rows(s, n=TOK):
         return pl.ds(aligned(s, TOK), n)
@@ -150,6 +164,15 @@
             back.at[a, h, rows(me)], outputs[a].at[:, head_columns(me, h)], back_local.at[h, a]
         )
 
+    def state_copy(i):
+        return pltpu.make_async_copy(states_in[i], state.at[i], state_sem.at[i])
+
+    def back_start(h):
+        for a in range(3):
+            back_own(h, a).start()
+            for p in range(3):
+                back_copy(h, a, p).start()
+
     cot_own().start()
     w_own().start()
     for c in range(CC):
@@ -163,6 +186,8 @@
             for p in range(3):
                 head_send(h, a, p).start()
 
+    for i in range(4):
+        state_copy(i).start()
     for c in range(CC):
         cot_cross(c).wait_recv()
         cot_forward(c).start()
@@ -274,14 +299,20 @@
                 head_own(h, a).wait()
                 for p in range(3):
                     head_recv(h, a, p).wait_recv()
+
+            @pl.when(h == HD - 1)
+            def _():
+                @pl.loop(0, HD - 1)
+                def _(g):
+                    back_start(g)
+
             compute(h)
             for p in range(3):
                 first_x(h, p).start()
                 first_z(h, p).start()
-            for a in range(3):
-                back_own(h, a).start()
-                for p in range(3):
-                    back_copy(h, a, p).start()
+            @pl.when(h == HD - 1)
+            def _():
+                back_start(HD - 1)
 
         @pl.when((h >= 1) & (h <= HD))
         def _():
@@ -296,7 +327,128 @@
         third(h).wait_recv()
         total = (k3[h] + r3[h].astype(F32)).astype(BF)
         for c in range(5):
-            rs_out[h * 5 + c] = total[:, c * 128 : (c + 1) * 128]
+            g_all[z, h * 5 + c] = total[:, c * 128 : (c + 1) * 128]
+
+    r = 2 * x + yh
+
+    def member(k):
+        j = lax.rem(r + k, 8)
+        return j, dp_index(j // 2, z, lax.rem(j, 2))
+
+    def gather_g(p):
+        device = dp_index(x, ring(z, p + 1), yh)
+        return remote(g_all.at[z], g_all.at[z], g_send.at[p], g_recv.at[p], (device, me))
+
+    for p in range(3):
+        gather_g(p).start()
+    for p in range(3):
+        gather_g(p).wait_recv()
+
+    def to_owner(k):
+        j, device = member(k)
+        return remote(tx.at[j], rx.at[r], t_send.at[k - 1], t_recv.at[k - 1], (device, me))
+
+    for k in range(1, 8):
+        j, device = member(k)
+        for s in range(SL):
+            source = slot_from[device * SL + s]
+            tx[j, s] = g_all[source // 25, lax.rem(source, 25)]
+        to_owner(k).start()
+    for s in range(SL):
+        source = slot_from[dp * SL + s]
+        rx[r, s] = g_all[source // 25, lax.rem(source, 25)]
+    for i in range(4):
+        state_copy(i).wait()
+    for k in range(1, 8):
+        to_owner(k).wait_recv()
+
+    def state_out(i):
+        return pltpu.make_async_copy(state.at[i], states_out[i], state_out_sem.at[i])
+
+    even = None
+    for s in range(SL):
+        gradient = rx[:, s].astype(F32).reshape(128, 128) * (1.0 / 32.0)
+        before = [state[i, s] for i in range(4)]
+        stepped = adam_step(*before, gradient)
+        keep = jnp.full((128, 128), filled[dp], jnp.int32) > s
+        after = [jnp.where(keep, new, old) for new, old in zip(stepped, before)]
+        for i in range(4):
+            state[i, s] = after[i]
+        fresh = after[0].reshape(16, 8, 128)
+        if s % 2 == 0:
+            even = fresh
+        if s % 2 == 1 or s == SL - 1:
+            pieces[:, s // 2] = jnp.concatenate([even, fresh], axis=1).astype(BF)
+    mine = 4 * x + z
+
+    def from_owner(k):
+        device = lax.rem(dp + k, 32)
+        return remote(pieces.at[device // 2], landed.at[dp], n_send.at[k - 1], n_recv.at[k - 1], (device, me))
+
+    for k in range(1, 32):
+        from_owner(k).start()
+    for i in range(4):
+        state_out(i).start()
+    landed[dp] = pieces[mine]
+    for k in range(1, 32):
+        from_owner(k).wait_recv()
+
+    for pair in range(50):
+        halves = []
+        for b in (2 * pair, 2 * pair + 1):
+            source = block_from[b]
+            tile = landed[source // 8, lax.rem(source, 8) // 2].astype(F32)
+            odd = jnp.full((8, 128), lax.rem(source, 2), jnp.int32) == 1
+            halves.append(jnp.where(odd, tile[8:], tile[:8]))
+        w16[x, z, pair] = jnp.concatenate(halves, axis=0).astype(BF)
+
+    near, far = pl.ds(0, 25), pl.ds(25, 25)
+
+    def gather_x(p, i, part, send, recv):
+        place = w16.at[x, ring(z, i), part]
+        return remote(place, place, send.at[p, i], recv.at[p, i], (dp_index(ring(x, p + 1), z, yh), me))
+
+    def gather_z(p, i, part, send, recv):
+        place = w16.at[ring(x, i), z, part]
+        return remote(place, place, send.at[p, i], recv.at[p, i], (dp_index(x, ring(z, p + 1), yh), me))
+
+    def landed_x(p, i, part, send, recv):
+        place = w16.at[ring(x, 3 - p), ring(z, i), part]
+        return remote(place, place, send.at[p, i], recv.at[p, i], (dp_index(ring(x, 3 - p), z, yh), me))
+
+    def landed_z(p, i, part, send, recv):
+        place = w16.at[ring(x, i), ring(z, 3 - p), part]
+        return remote(place, place, send.at[p, i], recv.at[p, i], (dp_index(x, ring(z, 3 - p), yh), me))
+
+    ax, az = (a_send.at[0], a_recv.at[0]), (a_send.at[1], a_recv.at[1])
+    bx, bz = (b_send.at[0], b_recv.at[0]), (b_send.at[1], b_recv.at[1])
+    for p in range(3):
+        gather_x(p, 0, near, *ax).start()
+        gather_z(p, 0, far, *bz).start()
+    for p in range(3):
+        gather_z(p, 0, near, *az).start()
+        gather_x(p, 0, far, *bx).start()
+    for i in range(3):
+        landed_x(i, 0, near, *ax).wait_recv()
+        landed_z(i, 0, far, *bz).wait_recv()
+        for p in range(3):
+            gather_z(p, 3 - i, near, *az).start()
+            gather_x(p, 3 - i, far, *bx).start()
+    for p in range(3):
+        for i in range(4):
+            landed_z(p, i, near, *az).wait_recv()
+            landed_x(p, i, far, *bx).wait_recv()
+
+    @pl.loop(0, HD)
+    def _(h):
+        for c in range(10):
+            for j in range(8):
+                low = w16[j // 2, 2 * (j % 2), h * 10 + c].astype(F32)
+                high = w16[j // 2, 2 * (j % 2) + 1, h * 10 + c].astype(F32)
+                left = jnp.concatenate([low[:8], high[:8]], axis=0)
+                right = jnp.concatenate([low[8:], high[8:]], axis=0)
+                w_out[h, j * 16 : (j + 1) * 16, c * 256 : c * 256 + 128] = left.astype(BF)
+                w_out[h, j * 16 : (j + 1) * 16, c * 256 + 128 : c * 256 + 256] = right.astype(BF)
 
     for c in range(CC):
         cot_cross(c).wait_send()
@@ -318,16 +470,32 @@
                 back_copy(h, a, p).wait_send()
                 back_recv_copy(h, a, p).wait_recv()
 
-
-def attend(q, k, v, cot, w, bias):
+    for p in range(3):
+        gather_g(p).wait_send()
+        gather_x(p, 0, near, *ax).wait_send()
+        gather_z(p, 0, far, *bz).wait_send()
+        for i in range(4):
+            gather_z(p, i, near, *az).wait_send()
+            gather_x(p, i, far, *bx).wait_send()
+    for k in range(1, 8):
+        to_owner(k).wait_send()
+    for k in range(1, 32):
+        from_owner(k).wait_send()
+    for i in range(4):
+        state_out(i).wait()
+
+
+def step(q, k, v, cot, w, bias, slot_from, filled, block_from, *states):
     any_space = pl.BlockSpec(memory_space=pl.ANY)
     vmem = pl.BlockSpec(memory_space=pltpu.VMEM)
+    smem = pl.BlockSpec(memory_space=pltpu.SMEM)
     sems = lambda *shape: pltpu.SemaphoreType.DMA(shape)
     return pl.pallas_call(
-        attend_kernel,
-        out_shape=[jax.ShapeDtypeStruct((TOK, OUTW), BF)] * 3 + [jax.ShapeDtypeStruct((25, 16, 128), BF)],
-        in_specs=[any_space] * 5 + [vmem],
-        out_specs=[any_space] * 3 + [vmem],
+        step_kernel,
+        out_shape=[jax.ShapeDtypeStruct((TOK, OUTW), BF)] * 3 + [jax.ShapeDtypeStruct((HD, 128, OUTW), BF)]
+        + [jax.ShapeDtypeStruct((SL, 128, 128), F32)] * 4,
+        in_specs=[any_space] * 5 + [vmem] + [smem] * 3 + [any_space] * 4,
+        out_specs=[any_space] * 3 + [vmem] + [any_space] * 4,
         scratch_shapes=[
             pltpu.VMEM((3, HD, LEN, 128), BF),
             pltpu.VMEM((LEN, OUTW), BF),
@@ -358,146 +526,30 @@
             *([sems(HD, 3)] * 8),
             sems(HD),
             sems(HD),
+            pltpu.VMEM((4, SL, 128, 128), F32),
+            pltpu.VMEM((4, 25, 16, 128), BF),
+            pltpu.VMEM((8, SL, 16, 128), BF),
+            pltpu.VMEM((8, SL, 16, 128), BF),
+            pltpu.VMEM((16, 4, 16, 128), BF),
+            pltpu.VMEM((32, 4, 16, 128), BF),
+            pltpu.VMEM((4, 4, 50, 16, 128), BF),
+            sems(4),
+            sems(4),
+            sems(3),
+            sems(3),
+            sems(7),
+            sems(7),
+            sems(31),
+            sems(31),
+            sems(2, 3, 4),
+            sems(2, 3, 4),
+            sems(2, 3, 4),
+            sems(2, 3, 4),
         ],
         compiler_params=pltpu.CompilerParams(
             collective_id=0, has_side_effects=True, vmem_limit_bytes=56 * 1024 * 1024
         ),
-    )(q, k, v, cot, w, bias)
-
-
-def adam_step(master_in, first_in, second_in, mean_in, gradient):
-    first_out = beta_one * first_in + (1.0 - beta_one) * gradient
-    second_out = beta_two * second_in + (1.0 - beta_two) * gradient * gradient
-    direction = first_out / bias_one / (jnp.sqrt(second_out / bias_two) + adam_eps)
-    master_out = master_in - learn_rate * (direction + weight_decay * master_in)
-    mean_out = ema_keep * mean_in + (1.0 - ema_keep) * master_out
-    return (master_out, first_out, second_out, mean_out)
-
-
-def update_kernel(
-    rs, slot_from, filled, block_from, master, one, two, mean,
-    w_out, master_out, one_out, two_out, mean_out,
-    g_all, tx, rx, nb, t_all, nw,
-    own_sem, g_send, g_recv, t_send, t_recv, n_send, n_recv, a_send, a_recv, w_send, w_recv,
-):
-    dp, me, x, z, yh = place_of()
-    r = 2 * x + yh
-
-    def member(k):
-        j = lax.rem(r + k, 8)
-        return j, dp_index(j // 2, z, lax.rem(j, 2))
-
-    def z_peer(p):
-        return dp_index(x, ring(z, p + 1), yh)
-
-    barrier = pltpu.get_barrier_semaphore()
-    for p in range(3):
-        pl.semaphore_signal(barrier, inc=1, device_id=(z_peer(p), me), device_id_type=MESH)
-    for k in range(1, 8):
-        pl.semaphore_signal(barrier, inc=1, device_id=(member(k)[1], me), device_id_type=MESH)
-    pl.semaphore_wait(barrier, 10)
-
-    g_all[z] = rs[...]
-
-    def gather_g(p):
-        return remote(rs, g_all.at[z], g_send.at[p], g_recv.at[p], (z_peer(p), me))
-
-    for p in range(3):
-        gather_g(p).start()
-    for p in range(3):
-        gather_g(p).wait_recv()
-
-    def to_owner(k):
-        j, device = member(k)
-        return remote(tx.at[j], rx.at[r], t_send.at[k - 1], t_recv.at[k - 1], (device, me))
-
-    for k in range(1, 8):
-        j, device = member(k)
-        for s in range(SL):
-            source = slot_from[device * SL + s]
-            tx[j, s] = g_all[source // 25, lax.rem(source, 25)]
-        to_owner(k).start()
-    for s in range(SL):
-        source = slot_from[dp * SL + s]
-        rx[r, s] = g_all[source // 25, lax.rem(source, 25)]
-    for k in range(1, 8):
-        to_owner(k).wait_recv()
-
-    for s in range(SL):
-        gradient = rx[:, s].astype(F32).reshape(128, 128) * (1.0 / 32.0)
-        before = (master[s], one[s], two[s], mean[s])
-        stepped = adam_step(*before, gradient)
-        keep = jnp.full((128, 128), filled[dp], jnp.int32) > s
-        after = [jnp.where(keep, new, old) for new, old in zip(stepped, before)]
-        master_out[s], one_out[s], two_out[s], mean_out[s] = after
-        nb[:, s] = after[0].astype(BF).reshape(8, 16, 128)
-
-    def from_owner(k):
-        j, device = member(k)
-        return remote(nb.at[j], t_all.at[z, r], n_send.at[k - 1], n_recv.at[k - 1], (device, me))
-
-    for k in range(1, 8):
-        from_owner(k).start()
-    t_all[z, r] = nb[r]
-    for k in range(1, 8):
-        from_owner(k).wait_recv()
-
-    def gather_t(p):
-        return remote(t_all.at[z], t_all.at[z], a_send.at[p], a_recv.at[p], (z_peer(p), me))
-
-    for p in range(3):
-        gather_t(p).start()
-    for p in range(3):
-        gather_t(p).wait_recv()
-
-    for h in range(HD):
-        for c in range(20):
-            source = block_from[h * 20 + c]
-            nw[h, :, c * 128 : (c + 1) * 128] = t_all[source // 56, lax.rem(source // 7, 8), lax.rem(source, 7)]
-
-    def gather_w(k):
-        return remote(nw, w_out.at[:, r], w_send.at[k - 1], w_recv.at[k - 1], (member(k)[1], me))
-
-    own = pltpu.make_async_copy(nw, w_out.at[:, r], own_sem)
-    for k in range(1, 8):
-        gather_w(k).start()
-    own.start()
-    for k in range(1, 8):
-        gather_w(k).wait_recv()
-    own.wait()
-    for p in range(3):
-        gather_g(p).wait_send()
-        gather_t(p).wait_send()
-    for k in range(1, 8):
-        to_owner(k).wait_send()
-        from_owner(k).wait_send()
-        gather_w(k).wait_send()
-
-
-def update(rs, slot_from, filled, block_from, master, one, two, mean):
-    any_space = pl.BlockSpec(memory_space=pl.ANY)
-    vmem = pl.BlockSpec(memory_space=pltpu.VMEM)
-    smem = pl.BlockSpec(memory_space=pltpu.SMEM)
-    sems = lambda *shape: pltpu.SemaphoreType.DMA(shape)
-    return pl.pallas_call(
-        update_kernel,
-        out_shape=[jax.ShapeDtypeStruct((HD, 8, 16, OUTW), BF)] + [jax.ShapeDtypeStruct((SL, 128, 128), F32)] * 4,
-        in_specs=[vmem, smem, smem, smem] + [vmem] * 4,
-        out_specs=[any_space] + [vmem] * 4,
-        scratch_shapes=[
-            pltpu.VMEM((4, 25, 16, 128), BF),
-            pltpu.VMEM((8, SL, 16, 128), BF),
-            pltpu.VMEM((8, SL, 16, 128), BF),
-            pltpu.VMEM((8, SL, 16, 128), BF),
-            pltpu.VMEM((4, 8, SL, 16, 128), BF),
-            pltpu.VMEM((HD, 16, OUTW), BF),
-            pltpu.SemaphoreType.DMA,
-            sems(3), sems(3), sems(7), sems(7), sems(7), sems(7), sems(3), sems(3), sems(7), sems(7),
-        ],
-        compiler_params=pltpu.CompilerParams(
-            collective_id=1, has_side_effects=True, vmem_limit_bytes=32 * 1024 * 1024
-        ),
-    )(rs, slot_from, filled, block_from, master, one, two, mean)
+    )(q, k, v, cot, w, bias, slot_from, filled, block_from, *states)
 
 
 def local(q, k, v, cot, w, tile_list, owners, master, one, two, mean):
@@ -516,12 +568,12 @@
     lies_at = (column // 5) * 25 + head * 5 + column % 5
     match = (group[None, None, :] == data[:, None, None]) & (slot_of[None, None, :] == slots[None, :, None])
     slot_from = jnp.sum(jnp.where(match, lies_at[None, None, :], 0), axis=2).reshape(-1)
-    plane = (group // 2) % 4
-    block_from = (plane * 8 + (group // 8) * 2 + group % 2) * SL + slot_of
-
-    dq, dk, dv, rs = attend(q, k, v, cot, w, bias)
-    new_w, *state = update(rs, slot_from, filled, block_from, master[0], one[0], two[0], mean[0])
-    return (dq, dk, dv, new_w.reshape(HD * 128, OUTW), *[s[None] for s in state])
+    block_from = group * 8 + slot_of
+
+    dq, dk, dv, new_w, *states = step(
+        q, k, v, cot, w, bias, slot_from, filled, block_from, master[0], one[0], two[0], mean[0]
+    )
+    return (dq, dk, dv, new_w.reshape(HD * 128, OUTW), *[s[None] for s in states])
 
 
 def solution(mesh):

time: 224 us -> 200 us (0.89)
  the two profiles are of different devices: /device:TPU:52 before, /device:TPU:0 now
where the time goes in v2:
time: 200 us; the launch traced here: 199 us
  Pallas kernels  183 us (92%)
  local copies, waits for them, and re-layouts  13.3 us (7%)
  other arithmetic  2.41 us (1%)
    pallas_call x1, Pallas kernels, step(): pl.pallas_call(step_kernel, out_shape=[jax.ShapeDtypeStruct((TOK, OUTW),...  183 us
    unnamed x23, local copies, waits for them, and re-layouts  11 us

profile of v2, /device:TPU:0, one launch (start us, length us, event | category | flops | bytes accessed | tf_op | source)
XLA Modules:
  0.0 199.3 jit_solution(1112733105237835275)
XLA Ops:
  0.6 0.8 dynamic-slice_bitcast_fusion
  1.4 0.2 convert_reduce_fusion
  1.6 1.3 multiply_add_fusion.block_from
  2.9 0.6 convert_reduce_fusion.1.filled
  3.5 0.2 select_reduce_fusion
  3.7 0.8 copy.19
  4.5 0.1 fusion.1
  4.6 0.1 copy.20
  4.7 0.7 reshape.120.slot_from
  5.4 0.7 broadcast_bitcast_fusion.bias
  6.0 183.0 %shard_map.170 = (bf16[256,2560]{1,0:T(8,128)(2,1)}, bf16[256,2560]{1,0:T(8,128)(2,1)}, bf16[256,2560]{1,0:T(8,128)(2,1)}, bf16[5,128,2560]{2,1,0:T(8,128)(2,1)}...) custom-call(bf16[256,2560]{1,0:T(8,128)(2,1)} %q_in.1, ...), custom_call_target="tpu_custom_call" | custom-call | tf_op jit(solution)/shard_map/pallas_call | solution.py:493
  189.0 0.0 copy-start.2
  189.0 0.0 copy-start.1
  189.1 2.6 %copy.29 = bf16[256,2560]{1,0:T(8,128)(2,1)} copy(bf16[256,2560]{1,0:T(8,128)(2,1)} %get-tuple-element.32) | data formatting | bytes 2621440
  191.7 0.0 copy-done.2
  191.7 0.0 copy-start
  191.7 1.1 copy.30
  192.7 0.0 copy-done.1
  192.7 1.1 copy.31
  193.8 0.8 copy-done
  194.5 0.0 copy-start.6
  194.5 0.0 copy-start.5
  194.5 1.7 copy.32
  196.3 0.0 copy-done.6
  196.3 0.0 copy-start.4
  196.3 0.0 copy-start.3
  196.3 0.8 copy.33
  197.0 0.0 copy-done.5
  197.0 0.8 copy.34
  197.8 0.0 copy-done.4
  197.8 0.8 copy.35
  198.6 0.0 copy-done.3
  198.6 0.8 copy.36
  (4 shorter events, 0.0 us)
Async XLA Ops:
  189.0 2.6 %copy-start.2 = (bf16[256,2560]{1,0:T(8,128)(2,1)S(1)}, bf16[256,2560]{1,0:T(8,128)(2,1)}, u32[]{:S(2)}) copy-start(bf16[256,2560]{1,0:T(8,128)(2,1)} %get-tuple-element.33) | copy-start | bytes 3932164
  189.0 3.7 %copy-start.1 = (bf16[256,2560]{1,0:T(8,128)(2,1)S(1)}, bf16[256,2560]{1,0:T(8,128)(2,1)}, u32[]{:S(2)}) copy-start(bf16[256,2560]{1,0:T(8,128)(2,1)} %get-tuple-element.34) | copy-start | bytes 3932164
  191.7 2.9 %copy-start = (bf16[5,128,2560]{2,1,0:T(8,128)(2,1)S(1)}, bf16[5,128,2560]{2,1,0:T(8,128)(2,1)}, u32[]{:S(2)}) copy-start(bf16[5,128,2560]{2,1,0:T(8,128)(2,1)} %get-tuple-element.19) | copy-start | bytes 9830404
  194.5 1.7 copy-start.6
  194.5 2.5 %copy-start.5 = (f32[7,128,128]{2,1,0:T(8,128)S(1)}, f32[7,128,128]{2,1,0:T(8,128)}, u32[]{:S(2)}) copy-start(f32[7,128,128]{2,1,0:T(8,128)} %get-tuple-element.21) | copy-start | bytes 1376260
  196.3 1.5 copy-start.4
  196.3 2.3 %copy-start.3 = (f32[7,128,128]{2,1,0:T(8,128)S(1)}, f32[7,128,128]{2,1,0:T(8,128)}, u32[]{:S(2)}) copy-start(f32[7,128,128]{2,1,0:T(8,128)} %get-tuple-element.23) | copy-start | bytes 1376260

commit v3 on v2

v3 whole, which is shorter than its diff:
```python
import math

import jax
import jax.numpy as jnp
from jax import lax
from jax.experimental import pallas as pl
from jax.experimental.pallas import tpu as pltpu
from jax.sharding import PartitionSpec as P

MESH = pl.DeviceIdType.MESH
BF = jnp.bfloat16
F32 = jnp.float32

learn_rate = 0.001
beta_one = 0.9
beta_two = 0.95
adam_eps = 1e-08
weight_decay = 0.1
ema_keep = 0.99
bias_one = 1.0 - (0.9**50) ** 2
bias_two = 1.0 - (0.95**50) ** 2

HD = 5
TOK = 256
LEN = 1024
OUTW = 2560
SL = 7
NEG = -1e30
SCALE = 1.0 / math.sqrt(128.0)
SCALE2 = SCALE * math.log2(math.e)
BACK_ONE, BACK_TWO = 6, 8
CC = 4


def aligned(value, step):
    return pl.multiple_of(value * step, step)


def remote(src, dst, send, recv, device):
    return pltpu.make_async_remote_copy(
        src_ref=src, dst_ref=dst, send_sem=send, recv_sem=recv, device_id=device, device_id_type=MESH
    )


def dot(a, b):
    return lax.dot_general(a, b, (((1,), (0,)), ((), ())), preferred_element_type=F32)


def dot_nt(a, b):
    return lax.dot_general(a, b, (((1,), (1,)), ((), ())), preferred_element_type=F32)


def place_of():
    dp = lax.axis_index("dp")
    return dp, lax.axis_index("seq"), dp // 8, (dp // 2) % 4, dp % 2


def dp_index(x, z, yh):
    return (x * 4 + z) * 2 + yh


def ring(value, step):
    return lax.rem(value + step, 4)


def adam_step(master_in, first_in, second_in, mean_in, gradient):
    first_out = beta_one * first_in + (1.0 - beta_one) * gradient
    second_out = beta_two * second_in + (1.0 - beta_two) * gradient * gradient
    direction = first_out / bias_one / (jnp.sqrt(second_out / bias_two) + adam_eps)
    master_out = master_in - learn_rate * (direction + weight_decay * master_in)
    mean_out = ema_keep * mean_in + (1.0 - ema_keep) * master_out
    return (master_out, first_out, second_out, mean_out)


def step_kernel(
    q_in, k_in, v_in, cot_in, w_in, tile_list, owners, *refs,
):
    states_in, refs = refs[:4], refs[4:]
    dq_out, dk_out, dv_out, w_out = refs[:4]
    states_out, refs = refs[4:8], refs[8:]
    (
    qkv, cot, w, da, back, kt, vt, att, probs, dk_acc, dv_acc,
    gx, gz, r1x, r1z, s2x, s2z, r2x, r2z, sums,
    local_sem, back_local, cot_send, cot_recv, in_send, in_recv, back_send, back_recv,
    x1_send, x1_recv, z1_send, z1_recv, x2_send, x2_recv, z2_send, z2_recv,
    state, tx, rx, pieces, landed, w16,
    state_sem, state_out_sem, t_send, t_recv, n_send, n_recv,
    a_send, a_recv, b_send, b_recv,
    bias, slot_table, block_table, slot_from, block_from, table_sem,
    ) = refs
    dp, me, x, z, yh = place_of()
    sibling = me + 1 - 2 * lax.rem(me, 2)
    across = ring(me, 2)
    corner = ring(sibling, 2)
    peers = [ring(me, p) for p in (1, 2, 3)]
    sources = [ring(me, 4 - p) for p in (1, 2, 3)]
    inputs = (q_in, k_in, v_in)
    outputs = (dq_out, dk_out, dv_out)

    barrier = pltpu.get_barrier_semaphore()
    for t in peers:
        pl.semaphore_signal(barrier, inc=1, device_id=(dp, t), device_id_type=MESH)
    for k in range(1, 32):
        pl.semaphore_signal(barrier, inc=1, device_id=(lax.rem(dp + k, 32), me), device_id_type=MESH)
    pl.semaphore_wait(barrier, 34)

    def rows(s, n=TOK):
        return pl.ds(aligned(s, TOK), n)

    def cot_rows(s, c):
        return pl.ds(pl.multiple_of(s * TOK + c * (TOK // CC), TOK // CC), TOK // CC)

    def cot_cross(c):
        return remote(
            cot_in.at[pl.ds(c * (TOK // CC), TOK // CC)], cot.at[cot_rows(me, c)],
            cot_send.at[c], cot_recv.at[c], (dp, across),
        )

    def cot_sibling():
        return remote(cot_in, cot.at[rows(me)], cot_send.at[CC], cot_recv.at[CC], (dp, sibling))

    def cot_forward(c):
        part = cot.at[cot_rows(across, c)]
        return remote(part, part, cot_send.at[CC + 1 + c], cot_recv.at[CC + 1 + c], (dp, sibling))

    def cot_own():
        return pltpu.make_async_copy(cot_in, cot.at[rows(me)], local_sem.at[0])

    def w_own():
        return pltpu.make_async_copy(w_in, w, local_sem.at[1])

    def head_columns(t, h):
        return pl.ds(pl.multiple_of((t * HD + h) * 128, 128), 128)

    def head_send(h, a, p):
        t = peers[p]
        return remote(
            inputs[a].at[:, head_columns(t, h)], qkv.at[a, h, rows(me)],
            in_send.at[h, a, p], in_recv.at[h, a, p], (dp, t),
        )

    def head_recv(h, a, p):
        part = qkv.at[a, h, rows(sources[p])]
        return remote(part, part, in_send.at[h, a, p], in_recv.at[h, a, p], (dp, sources[p]))

    def head_own(h, a):
        return pltpu.make_async_copy(
            inputs[a].at[:, head_columns(me, h)], qkv.at[a, h, rows(me)], local_sem.at[2 + 3 * h + a]
        )

    def back_copy(h, a, p):
        t = peers[p]
        return remote(
            back.at[a, h, rows(t)], outputs[a].at[:, head_columns(me, h)],
            back_send.at[h, a, p], back_recv.at[h, a, p], (dp, t),
        )

    def back_recv_copy(h, a, p):
        return remote(
            back.at[a, h, rows(sources[p])], outputs[a].at[:, head_columns(sources[p], h)],
            back_send.at[h, a, p], back_recv.at[h, a, p], (dp, sources[p]),
        )

    def back_own(h, a):
        return pltpu.make_async_copy(
            back.at[a, h, rows(me)], outputs[a].at[:, head_columns(me, h)], back_local.at[h, a]
        )

    def state_copy(i):
        return pltpu.make_async_copy(states_in[i], state.at[i], state_sem.at[i])

    def back_start(first, last):
        @pl.loop(first, last)
        def _(unit):
            h, a = unit // 3, lax.rem(unit, 3)
            for i in range(3):

                @pl.when(a == i)
                def _():
                    back_own(h, i).start()
                    for p in range(3):
                        back_copy(h, i, p).start()

    cot_own().start()
    w_own().start()
    for c in range(CC):
        cot_cross(c).start()
    cot_sibling().start()

    @pl.loop(0, HD)
    def _(h):
        for a in range(3):
            head_own(h, a).start()
            for p in range(3):
                head_send(h, a, p).start()

    for i in range(4):
        state_copy(i).start()

    for i in range(8):
        for n in range(8):
            listed = tile_list[i, 0] == n
            for j in range(1, 6):
                listed = listed | (tile_list[i, j] == n)
            low = jnp.where(listed, 0.0, NEG).astype(F32)
            bias[i // 2, n : n + 1, (i % 2) * 128 : (i % 2) * 128 + 128] = jnp.full((1, 128), low, F32)

    lane = lax.broadcasted_iota(jnp.int32, (128, 128), 1)
    row = lax.broadcasted_iota(jnp.int32, (128, 128), 0)

    def put(b, held):
        return jnp.where(lane[:8] == b, owners[me * 100 + b], held)

    owner = lax.fori_loop(0, 100, put, jnp.full((8, 128), -1, jnp.int32))
    owner = jnp.broadcast_to(owner[:1], (128, 128))
    earlier = (owner.T == owner) & (row < lane)
    slot_of = jnp.sum(jnp.where(earlier, 1, 0), axis=0, keepdims=True)
    block_table[...] = jnp.broadcast_to(owner[:1] * 8 + slot_of, (8, 128))
    owned = owner[:32] == row[:32]
    for s in range(SL):
        match = owned & (jnp.broadcast_to(slot_of, (32, 128)) == s)
        block = jnp.sum(jnp.where(match, lane[:32], 0), axis=1, keepdims=True)
        slot_table[s] = jnp.broadcast_to(block, (32, 128))
    count = jnp.sum(jnp.where(owned, 1, 0), axis=1, keepdims=True)
    slot_table[SL] = jnp.broadcast_to(count, (32, 128))
    tables = (
        pltpu.make_async_copy(slot_table, slot_from, table_sem.at[0]),
        pltpu.make_async_copy(block_table, block_from, table_sem.at[1]),
    )
    for table in tables:
        table.start()
    for table in tables:
        table.wait()

    for c in range(CC):
        cot_cross(c).wait_recv()
        cot_forward(c).start()
    cot_own().wait()
    w_own().wait()
    cot_sibling().wait_recv()
    for c in range(CC):
        cot_forward(c).wait_recv()

    @pl.loop(0, 4)
    def _(b):
        d_rows = dot_nt(cot[pl.ds(aligned(b, 256), 256), :], w[...]).astype(BF)
        for h in range(HD):
            da[h, pl.ds(aligned(b, 256), 256), :] = d_rows[:, h * 128 : (h + 1) * 128]

    def forward(h):
        vt[...] = qkv[2, h].T
        for b in range(4):
            part = slice(b * 256, b * 256 + 256)
            score = dot_nt(qkv[1, h], qkv[0, h, part, :]).reshape(8, 128, 256) * SCALE2 + bias[b][:, None, :]
            score = score.reshape(LEN, 256)
            top = jnp.max(score, axis=0, keepdims=True)
            weight = jnp.exp2(score - top)
            total = jnp.sum(weight, axis=0, keepdims=True)
            prob = weight * (1.0 / total)
            probs[lax.rem(h, 2), b] = prob
            att[:, part] = dot(vt[...], prob.astype(BF)).astype(BF)

        @pl.loop(0, 2)
        def _(c):
            columns = pl.ds(aligned(c, 640), 640)
            grad = dot(att[...], cot[:, columns]).astype(BF)
            for xx in range(4):
                gx[h, xx, :, columns] = grad[xx * 32 : xx * 32 + 32]
            grad = dot(att[...], cot[:, pl.ds(pl.multiple_of(1280 + c * 640, 640), 640)])
            for zz in range(4):
                rows_z = [grad[a * 32 + zz * 8 : a * 32 + zz * 8 + 8] for a in range(4)]
                gz[h, zz, :, columns] = jnp.concatenate(rows_z, axis=0).astype(BF)

    def backward(h):
        kt[...] = qkv[1, h].T
        dk_acc[...] = jnp.zeros_like(dk_acc)
        dv_acc[...] = jnp.zeros_like(dv_acc)
        for b in range(4):
            part = slice(b * 256, b * 256 + 256)
            q_b = qkv[0, h, part, :]
            da_b = da[h, part, :]
            prob = probs[lax.rem(h, 2), b]
            d_prob = dot_nt(qkv[2, h], da_b)
            delta = jnp.sum(prob * d_prob, axis=0, keepdims=True)
            d_score = (prob * (d_prob - delta) * SCALE).astype(BF)
            back[0, h, part, :] = dot(kt[...], d_score).T.astype(BF)
            dk_acc[...] += dot(d_score, q_b)
            dv_acc[...] += dot(prob.astype(BF), da_b)

        back[1, h] = dk_acc[...].astype(BF)
        back[2, h] = dv_acc[...].astype(BF)

    def first_x(h, p):
        t = ring(x, p + 1)
        return remote(gx.at[h, t], r1x.at[h, p], x1_send.at[h, p], x1_recv.at[h, p], (dp_index(t, z, yh), me))

    def first_z(h, p):
        t = ring(z, p + 1)
        return remote(gz.at[h, t], r1z.at[h, p], z1_send.at[h, p], z1_recv.at[h, p], (dp_index(x, t, yh), me))

    def second_z(h, p):
        t = ring(z, p + 1)
        return remote(s2x.at[h, t], r2x.at[h, p], x2_send.at[h, p], x2_recv.at[h, p], (dp_index(x, t, yh), me))

    def second_x(h, p):
        t = ring(x, p + 1)
        return remote(s2z.at[h, t], r2z.at[h, p], z2_send.at[h, p], z2_recv.at[h, p], (dp_index(t, z, yh), me))

    def after_first(h):
        for p in range(3):
            first_x(h, p).wait_recv()
            first_z(h, p).wait_recv()
        total = gx[h, x].astype(F32)
        for p in range(3):
            total = total + r1x[h, p].astype(F32)
        for t in range(4):
            part = total[t * 8 : t * 8 + 8]
            s2x[h, t] = jnp.concatenate([part[:, :640], part[:, 640:]], axis=0).astype(BF)
        total = gz[h, z].astype(F32)
        for p in range(3):
            total = total + r1z[h, p].astype(F32)
        for t in range(4):
            part = total[t * 8 : t * 8 + 8]
            s2z[h, t] = jnp.concatenate([part[:, :640], part[:, 640:]], axis=0).astype(BF)
        for p in range(3):
            second_z(h, p).start()
            second_x(h, p).start()

    def after_second(h):
        for p in range(3):
            second_z(h, p).wait_recv()
            second_x(h, p).wait_recv()
        even = s2x[h, z].astype(F32)
        odd = s2z[h, x].astype(F32)
        for p in range(3):
            even = even + r2x[h, p].astype(F32)
            odd = odd + r2z[h, p].astype(F32)
        for i, total in enumerate((even, odd)):
            for u in range(2):
                for c in range(5):
                    sums[h * 20 + i * 10 + u * 5 + c] = total[u * 8 : u * 8 + 8, c * 128 : c * 128 + 128]

    @pl.loop(0, HD)
    def _(h):
        for a in range(3):
            head_own(h, a).wait()
            for p in range(3):
                head_recv(h, a, p).wait_recv()

        @pl.when(h == HD - 1)
        def _():
            back_start(0, BACK_ONE)

        forward(h)
        for p in range(3):
            first_x(h, p).start()
            first_z(h, p).start()

        @pl.when(h >= 1)
        def _():
            after_first(h - 1)
            backward(h - 1)
            after_second(h - 1)

    after_first(HD - 1)
    after_second(HD - 1)

    def pack(device):
        tiles = [sums[jnp.clip(slot_from[s, device, 0], 0, HD * 20 - 1)] for s in range(SL)]
        for t in range(4):
            tx[device, t] = jnp.concatenate([tiles[2 * t], tiles[min(2 * t + 1, SL - 1)]], axis=0).astype(BF)

    def to_owner(k):
        device = lax.rem(dp + k, 32)
        return remote(tx.at[device], rx.at[dp], t_send.at[k - 1], t_recv.at[k - 1], (device, me))

    @pl.loop(1, 32)
    def _(k):
        pack(lax.rem(dp + k, 32))
        to_owner(k).start()

    back_start(BACK_ONE, BACK_TWO)
    backward(HD - 1)
    pack(dp)
    rx[dp] = tx[dp]
    for i in range(4):
        state_copy(i).wait()

    @pl.loop(1, 32)
    def _(k):
        to_owner(k).wait_recv()

    def state_out(i):
        return pltpu.make_async_copy(state.at[i], states_out[i], state_out_sem.at[i])

    arrived = rx[...].reshape(16, 2, 4, 16, 128)
    even = None
    for s in range(SL):
        if s % 2 == 0:
            both = arrived[:, 0, s // 2].astype(F32) + arrived[:, 1, s // 2].astype(F32)
        half = both[:, :8] if s % 2 == 0 else both[:, 8:]
        gradient = half.reshape(128, 128) * (1.0 / 32.0)
        before = [state[i, s] for i in range(4)]
        stepped = adam_step(*before, gradient)
        keep = jnp.full((128, 128), slot_from[SL, dp, 0], jnp.int32) > s
        after = [jnp.where(keep, new, old) for new, old in zip(stepped, before)]
        for i in range(4):
            state[i, s] = after[i]
        fresh = after[0].reshape(16, 8, 128)
        if s % 2 == 0:
            even = fresh
        if s % 2 == 1 or s == SL - 1:
            pieces[:, s // 2] = jnp.concatenate([even, fresh], axis=1).astype(BF)
    mine = 4 * x + z

    def from_owner(k):
        device = lax.rem(dp + k, 32)
        return remote(pieces.at[device // 2], landed.at[dp], n_send.at[k - 1], n_recv.at[k - 1], (device, me))

    @pl.loop(1, 32)
    def _(k):
        from_owner(k).start()

    back_start(BACK_TWO, 3 * HD)
    for i in range(4):
        state_out(i).start()
    landed[dp] = pieces[mine]

    @pl.loop(1, 32)
    def _(k):
        from_owner(k).wait_recv()

    def arrange(pairs):
        for pair in pairs:
            halves = []
            for b in (2 * pair, 2 * pair + 1):
                source = jnp.clip(block_from[0, b], 0, 255)
                tile = landed[source // 8, lax.rem(source, 8) // 2].astype(F32)
                odd = jnp.full((8, 128), lax.rem(source, 2), jnp.int32) == 1
                halves.append(jnp.where(odd, tile[8:], tile[:8]))
            w16[x, z, pair] = jnp.concatenate(halves, axis=0).astype(BF)

    here = ((x, z), (z, x))

    def device_of(f, first, second):
        a, b = (first, second) if f == 0 else (second, first)
        return (dp_index(a, b, yh), me)

    def piece(f, first, second, d, kind):
        start, size = f * 25, 25
        if kind == 1:
            start, size = (start, 12) if d == 0 else (start + 12, 13)
        a, b = (first, second) if f == 0 else (second, first)
        return w16.at[a, b, pl.ds(start, size)]

    ways = (1, 3)

    def ring_one(f, d, kind):
        a, b = here[f]
        place = piece(f, a if kind == 0 else ring(a, ways[1 - d]), b, d, kind)
        return remote(place, place, a_send.at[f, d, kind], a_recv.at[f, d, kind], device_of(f, ring(a, ways[d]), b))

    def landed_one(f, d, kind):
        a, b = here[f]
        place = piece(f, ring(a, ways[1 - d]) if kind == 0 else ring(a, 2), b, d, kind)
        return remote(place, place, a_send.at[f, d, kind], a_recv.at[f, d, kind], device_of(f, ring(a, ways[1 - d]), b))

    def ring_two(f, i, d, kind):
        a, b = here[f]
        place = piece(f, ring(a, i), b if kind == 0 else ring(b, ways[1 - d]), d, kind)
        to = device_of(f, a, ring(b, ways[d]))
        return remote(place, place, b_send.at[f, i, d, kind], b_recv.at[f, i, d, kind], to)

    def landed_two(f, i, d, kind):
        a, b = here[f]
        place = piece(f, ring(a, i), ring(b, ways[1 - d]) if kind == 0 else ring(b, 2), d, kind)
        to = device_of(f, a, ring(b, ways[1 - d]))
        return remote(place, place, b_send.at[f, i, d, kind], b_recv.at[f, i, d, kind], to)

    both = [(f, d) for d in range(2) for f in range(2)]
    for f in range(2):
        arrange(range(f * 25, f * 25 + 25))
        for d in range(2):
            ring_one(f, d, 0).start()
        for d in range(2):
            ring_two(f, 0, d, 0).start()
    for f, d in both:
        landed_one(f, d, 0).wait_recv()
        ring_one(f, d, 1).start()
        for way in range(2):
            ring_two(f, ways[1 - d], way, 0).start()
    for f, d in both:
        landed_two(f, 0, d, 0).wait_recv()
        ring_two(f, 0, d, 1).start()
    for f, d in both:
        landed_one(f, d, 1).wait_recv()
    for f, d in both:
        ring_two(f, 2, d, 0).start()
    for i in (3, 1, 2):
        for f, d in both:
            landed_two(f, i, d, 0).wait_recv()
            ring_two(f, i, d, 1).start()
    for i in range(4):
        for f, d in both:
            landed_two(f, i, d, 1).wait_recv()

    @pl.loop(0, HD)
    def _(h):
        for c in range(10):
            for j in range(8):
                low = w16[j // 2, 2 * (j % 2), h * 10 + c].astype(F32)
                high = w16[j // 2, 2 * (j % 2) + 1, h * 10 + c].astype(F32)
                left = jnp.concatenate([low[:8], high[:8]], axis=0)
                right = jnp.concatenate([low[8:], high[8:]], axis=0)
                w_out[h, j * 16 : (j + 1) * 16, c * 256 : c * 256 + 128] = left.astype(BF)
                w_out[h, j * 16 : (j + 1) * 16, c * 256 + 128 : c * 256 + 256] = right.astype(BF)

    for c in range(CC):
        cot_cross(c).wait_send()
        cot_forward(c).wait_send()
    cot_sibling().wait_send()

    @pl.loop(0, HD)
    def _(h):
        for p in range(3):
            first_x(h, p).wait_send()
            first_z(h, p).wait_send()
            second_x(h, p).wait_send()
            second_z(h, p).wait_send()
        for a in range(3):
            back_own(h, a).wait()
            for p in range(3):
                head_send(h, a, p).wait_send()
                back_copy(h, a, p).wait_send()
                back_recv_copy(h, a, p).wait_recv()

    for f, d in both:
        for kind in range(2):
            ring_one(f, d, kind).wait_send()
            for i in range(4):
                ring_two(f, i, d, kind).wait_send()

    @pl.loop(1, 32)
    def _(k):
        to_owner(k).wait_send()
        from_owner(k).wait_send()

    for i in range(4):
        state_out(i).wait()


def step(q, k, v, cot, w, tile_list, owners, *states):
    any_space = pl.BlockSpec(memory_space=pl.ANY)
    vmem = pl.BlockSpec(memory_space=pltpu.VMEM)
    smem = pl.BlockSpec(memory_space=pltpu.SMEM)
    sems = lambda *shape: pltpu.SemaphoreType.DMA(shape)
    return pl.pallas_call(
        step_kernel,
        out_shape=[jax.ShapeDtypeStruct((TOK, OUTW), BF)] * 3 + [jax.ShapeDtypeStruct((HD, 128, OUTW), BF)]
        + [jax.ShapeDtypeStruct((SL, 128, 128), F32)] * 4,
        in_specs=[any_space] * 5 + [smem] * 2 + [any_space] * 4,
        out_specs=[any_space] * 3 + [vmem] + [any_space] * 4,
        scratch_shapes=[
            pltpu.VMEM((3, HD, LEN, 128), BF),
            pltpu.VMEM((LEN, OUTW), BF),
            pltpu.VMEM((HD * 128, OUTW), BF),
            pltpu.VMEM((HD, LEN, 128), BF),
            pltpu.VMEM((3, HD, LEN, 128), BF),
            pltpu.VMEM((128, LEN), BF),
            pltpu.VMEM((128, LEN), BF),
            pltpu.VMEM((128, LEN), BF),
            pltpu.VMEM((2, 4, LEN, 256), F32),
            pltpu.VMEM((LEN, 128), F32),
            pltpu.VMEM((LEN, 128), F32),
            pltpu.VMEM((HD, 4, 32, 1280), BF),
            pltpu.VMEM((HD, 4, 32, 1280), BF),
            pltpu.VMEM((HD, 3, 32, 1280), BF),
            pltpu.VMEM((HD, 3, 32, 1280), BF),
            pltpu.VMEM((HD, 4, 16, 640), BF),
            pltpu.VMEM((HD, 4, 16, 640), BF),
            pltpu.VMEM((HD, 3, 16, 640), BF),
            pltpu.VMEM((HD, 3, 16, 640), BF),
            pltpu.VMEM((HD * 20, 8, 128), F32),
            sems(2 + 3 * HD),
            sems(HD, 3),
            sems(2 * CC + 1),
            sems(2 * CC + 1),
            *([sems(HD, 3, 3)] * 4),
            *([sems(HD, 3)] * 8),
            pltpu.VMEM((4, SL, 128, 128), F32),
            pltpu.VMEM((32, 4, 16, 128), BF),
            pltpu.VMEM((32, 4, 16, 128), BF),
            pltpu.VMEM((16, 4, 16, 128), BF),
            pltpu.VMEM((32, 4, 16, 128), BF),
            pltpu.VMEM((4, 4, 50, 16, 128), BF),
            sems(4),
            sems(4),
            sems(31),
            sems(31),
            sems(31),
            sems(31),
            sems(2, 2, 2),
            sems(2, 2, 2),
            sems(2, 4, 2, 2),
            sems(2, 4, 2, 2),
            pltpu.VMEM((4, 8, 256), F32),
            pltpu.VMEM((8, 32, 128), jnp.int32),
            pltpu.VMEM((8, 128), jnp.int32),
            pltpu.SMEM((8, 32, 128), jnp.int32),
            pltpu.SMEM((8, 128), jnp.int32),
            sems(2),
        ],
        compiler_params=pltpu.CompilerParams(
            collective_id=0, has_side_effects=True, vmem_limit_bytes=56 * 1024 * 1024
        ),
    )(q, k, v, cot, w, tile_list, owners, *states)


def local(q, k, v, cot, w, tile_list, owners, master, one, two, mean):
    dq, dk, dv, new_w, *states = step(
        q, k, v, cot, w, tile_list, owners[:, 0], master[0], one[0], two[0], mean[0]
    )
    return (dq, dk, dv, new_w.reshape(HD * 128, OUTW), *[s[None] for s in states])


def solution(mesh):
    tokens = P(("dp", "seq"), None)
    state = P("dp", "seq", None, None)
    return jax.shard_map(
        local,
        mesh=mesh,
        in_specs=(tokens,) * 4 + (P("seq", None), P(), P()) + (state,) * 4,
        out_specs=(tokens,) * 3 + (P("seq", None),) + (state,) * 4,
        check_vma=False,
    )
```

time: 200 us -> 171 us (0.85)
  Pallas kernels: 183 us -> 160 us
  local copies, waits for them, and re-layouts: 13.3 us -> 10.3 us
  other arithmetic: 2.41 us -> 0 us
    pallas_call x1, Pallas kernels: 183 us -> 160 us  [step(): pl.pallas_call(step_kernel, out_shape=[jax.ShapeDtypeStruct((TOK, OUTW),...]
    unnamed x23 -> x22, local copies, waits for them, and re-layouts: 11 us -> 10.3 us
where the time goes in v3:
time: 171 us
  Pallas kernels  160 us (94%)
  local copies, waits for them, and re-layouts  10.3 us (6%)
    pallas_call x1, Pallas kernels, step(): pl.pallas_call(step_kernel, out_shape=[jax.ShapeDtypeStruct((TOK, OUTW),...  160 us
    unnamed x22, local copies, waits for them, and re-layouts  10.3 us

profile of v3, /device:TPU:0, one launch (start us, length us, event | category | flops | bytes accessed | tf_op | source)
XLA Modules:
  0.0 170.8 jit_solution(2794206156029303738)
XLA Ops:
  0.6 159.9 %shard_map.170 = (bf16[256,2560]{1,0:T(8,128)(2,1)}, bf16[256,2560]{1,0:T(8,128)(2,1)}, bf16[256,2560]{1,0:T(8,128)(2,1)}, bf16[5,128,2560]{2,1,0:T(8,128)(2,1)}...) custom-call(bf16[256,2560]{1,0:T(8,128)(2,1)} %q_in.1, ...), custom_call_target="tpu_custom_call" | custom-call | tf_op jit(solution)/shard_map/pallas_call | solution.py:557
  160.5 0.0 copy-start.2
  160.6 0.0 copy-start.1
  160.6 2.6 %copy.27 = bf16[256,2560]{1,0:T(8,128)(2,1)} copy(bf16[256,2560]{1,0:T(8,128)(2,1)} %get-tuple-element.32) | data formatting | bytes 2621440
  163.2 0.0 copy-done.2
  163.2 0.0 copy-start
  163.2 1.1 copy.28
  164.2 0.0 copy-done.1
  164.2 1.1 copy.29
  165.3 0.8 copy-done
  166.0 0.0 copy-start.6
  166.0 0.0 copy-start.5
  166.1 1.7 copy.30
  167.8 0.0 copy-done.6
  167.8 0.0 copy-start.4
  167.8 0.0 copy-start.3
  167.8 0.8 copy.31
  168.5 0.0 copy-done.5
  168.5 0.8 copy.32
  169.3 0.0 copy-done.4
  169.3 0.8 copy.33
  170.1 0.0 copy-done.3
  170.1 0.8 copy.34
Async XLA Ops:
  160.5 2.6 %copy-start.2 = (bf16[256,2560]{1,0:T(8,128)(2,1)S(1)}, bf16[256,2560]{1,0:T(8,128)(2,1)}, u32[]{:S(2)}) copy-start(bf16[256,2560]{1,0:T(8,128)(2,1)} %get-tuple-element.33) | copy-start | bytes 3932164
  160.6 3.7 %copy-start.1 = (bf16[256,2560]{1,0:T(8,128)(2,1)S(1)}, bf16[256,2560]{1,0:T(8,128)(2,1)}, u32[]{:S(2)}) copy-start(bf16[256,2560]{1,0:T(8,128)(2,1)} %get-tuple-element.34) | copy-start | bytes 3932164
  163.2 2.9 %copy-start = (bf16[5,128,2560]{2,1,0:T(8,128)(2,1)S(1)}, bf16[5,128,2560]{2,1,0:T(8,128)(2,1)}, u32[]{:S(2)}) copy-start(bf16[5,128,2560]{2,1,0:T(8,128)(2,1)} %get-tuple-element.19) | copy-start | bytes 9830404
  166.0 1.7 %copy-start.6 = (f32[7,128,128]{2,1,0:T(8,128)S(1)}, f32[7,128,128]{2,1,0:T(8,128)}, u32[]{:S(2)}) copy-start(f32[7,128,128]{2,1,0:T(8,128)} %get-tuple-element.20) | copy-start | bytes 1376260
  166.0 2.5 %copy-start.5 = (f32[7,128,128]{2,1,0:T(8,128)S(1)}, f32[7,128,128]{2,1,0:T(8,128)}, u32[]{:S(2)}) copy-start(f32[7,128,128]{2,1,0:T(8,128)} %get-tuple-element.21) | copy-start | bytes 1376260
  167.8 1.5 copy-start.4
  167.8 2.3 %copy-start.3 = (f32[7,128,128]{2,1,0:T(8,128)S(1)}, f32[7,128,128]{2,1,0:T(8,128)}, u32[]{:S(2)}) copy-start(f32[7,128,128]{2,1,0:T(8,128)} %get-tuple-element.23) | copy-start | bytes 1376260

commit v4 on v3

--- a/solution.py
+++ b/solution.py
@@ -79,14 +79,14 @@
     dq_out, dk_out, dv_out, w_out = refs[:4]
     states_out, refs = refs[4:8], refs[8:]
     (
-    qkv, cot, w, da, back, kt, vt, att, probs, dk_acc, dv_acc,
+    qkv, cot, w, da, back, kt, vt, att, probs, weights, scale_row, dk_acc, dv_acc,
     gx, gz, r1x, r1z, s2x, s2z, r2x, r2z, sums,
     local_sem, back_local, cot_send, cot_recv, in_send, in_recv, back_send, back_recv,
     x1_send, x1_recv, z1_send, z1_recv, x2_send, x2_recv, z2_send, z2_recv,
     state, tx, rx, pieces, landed, w16,
     state_sem, state_out_sem, t_send, t_recv, n_send, n_recv,
     a_send, a_recv, b_send, b_recv,
-    bias, slot_table, block_table, slot_from, block_from, table_sem,
+    bias, slot_table, block_table, slot_from, block_from, table_sem, w_new, w_sem,
     ) = refs
     dp, me, x, z, yh = place_of()
     sibling = me + 1 - 2 * lax.rem(me, 2)
@@ -247,18 +247,23 @@
         for h in range(HD):
             da[h, pl.ds(aligned(b, 256), 256), :] = d_rows[:, h * 128 : (h + 1) * 128]
 
-    def forward(h):
+    def scores(h):
+        for b in range(4):
+            part = slice(b * 256, b * 256 + 256)
+            score = dot_nt(qkv[1, h], qkv[0, h, part, :]).reshape(8, 128, 256)
+            top = jnp.max(jnp.max(score, axis=1) * SCALE2 + bias[b], axis=0, keepdims=True)
+            shift = top - bias[b]
+            weight = jnp.exp2(score * SCALE2 - shift[:, None, :]).reshape(LEN, 256)
+            total = jnp.sum(weight, axis=0, keepdims=True)
+            probs[lax.rem(h, 2), b] = weight
+            weights[b] = weight.astype(BF)
+            scale_row[lax.rem(h, 2), b] = jnp.broadcast_to(1.0 / total, (8, 256))
+
+    def weight_grad(h):
         vt[...] = qkv[2, h].T
         for b in range(4):
             part = slice(b * 256, b * 256 + 256)
-            score = dot_nt(qkv[1, h], qkv[0, h, part, :]).reshape(8, 128, 256) * SCALE2 + bias[b][:, None, :]
-            score = score.reshape(LEN, 256)
-            top = jnp.max(score, axis=0, keepdims=True)
-            weight = jnp.exp2(score - top)
-            total = jnp.sum(weight, axis=0, keepdims=True)
-            prob = weight * (1.0 / total)
-            probs[lax.rem(h, 2), b] = prob
-            att[:, part] = dot(vt[...], prob.astype(BF)).astype(BF)
+            att[:, part] = (dot(vt[...], weights[b]) * scale_row[lax.rem(h, 2), b, :1]).astype(BF)
 
         @pl.loop(0, 2)
         def _(c):
@@ -279,15 +284,17 @@
             part = slice(b * 256, b * 256 + 256)
             q_b = qkv[0, h, part, :]
             da_b = da[h, part, :]
-            prob = probs[lax.rem(h, 2), b]
+            inverse = scale_row[lax.rem(h, 2), b, :1]
+            weight = probs[lax.rem(h, 2), b]
             d_prob = dot_nt(qkv[2, h], da_b)
-            delta = jnp.sum(prob * d_prob, axis=0, keepdims=True)
-            d_score = (prob * (d_prob - delta) * SCALE).astype(BF)
-            back[0, h, part, :] = dot(kt[...], d_score).T.astype(BF)
+            delta = jnp.sum(weight * d_prob, axis=0, keepdims=True) * inverse
+            prob = weight * inverse
+            d_score = (prob * (d_prob - delta)).astype(BF)
+            back[0, h, part, :] = (dot(kt[...], d_score) * SCALE).T.astype(BF)
             dk_acc[...] += dot(d_score, q_b)
             dv_acc[...] += dot(prob.astype(BF), da_b)
 
-        back[1, h] = dk_acc[...].astype(BF)
+        back[1, h] = (dk_acc[...] * SCALE).astype(BF)
         back[2, h] = dv_acc[...].astype(BF)
 
     def first_x(h, p):
@@ -342,16 +349,21 @@
 
     @pl.loop(0, HD)
     def _(h):
-        for a in range(3):
+        def arrive(a):
             head_own(h, a).wait()
             for p in range(3):
                 head_recv(h, a, p).wait_recv()
 
+        arrive(0)
+        arrive(1)
+
         @pl.when(h == HD - 1)
         def _():
             back_start(0, BACK_ONE)
 
-        forward(h)
+        scores(h)
+        arrive(2)
+        weight_grad(h)
         for p in range(3):
             first_x(h, p).start()
             first_z(h, p).start()
@@ -504,6 +516,9 @@
         for f, d in both:
             landed_two(f, i, d, 1).wait_recv()
 
+    def w_copy(h):
+        return pltpu.make_async_copy(w_new.at[h], w_out.at[h], w_sem.at[h])
+
     @pl.loop(0, HD)
     def _(h):
         for c in range(10):
@@ -512,8 +527,9 @@
                 high = w16[j // 2, 2 * (j % 2) + 1, h * 10 + c].astype(F32)
                 left = jnp.concatenate([low[:8], high[:8]], axis=0)
                 right = jnp.concatenate([low[8:], high[8:]], axis=0)
-                w_out[h, j * 16 : (j + 1) * 16, c * 256 : c * 256 + 128] = left.astype(BF)
-                w_out[h, j * 16 : (j + 1) * 16, c * 256 + 128 : c * 256 + 256] = right.astype(BF)
+                w_new[h, j * 16 : (j + 1) * 16, c * 256 : c * 256 + 128] = left.astype(BF)
+                w_new[h, j * 16 : (j + 1) * 16, c * 256 + 128 : c * 256 + 256] = right.astype(BF)
+        w_copy(h).start()
 
     for c in range(CC):
         cot_cross(c).wait_send()
@@ -547,11 +563,12 @@
 
     for i in range(4):
         state_out(i).wait()
+    for h in range(HD):
+        w_copy(h).wait()
 
 
 def step(q, k, v, cot, w, tile_list, owners, *states):
     any_space = pl.BlockSpec(memory_space=pl.ANY)
-    vmem = pl.BlockSpec(memory_space=pltpu.VMEM)
     smem = pl.BlockSpec(memory_space=pltpu.SMEM)
     sems = lambda *shape: pltpu.SemaphoreType.DMA(shape)
     return pl.pallas_call(
@@ -559,7 +576,7 @@
         out_shape=[jax.ShapeDtypeStruct((TOK, OUTW), BF)] * 3 + [jax.ShapeDtypeStruct((HD, 128, OUTW), BF)]
         + [jax.ShapeDtypeStruct((SL, 128, 128), F32)] * 4,
         in_specs=[any_space] * 5 + [smem] * 2 + [any_space] * 4,
-        out_specs=[any_space] * 3 + [vmem] + [any_space] * 4,
+        out_specs=[any_space] * 8,
         scratch_shapes=[
             pltpu.VMEM((3, HD, LEN, 128), BF),
             pltpu.VMEM((LEN, OUTW), BF),
@@ -570,6 +587,8 @@
             pltpu.VMEM((128, LEN), BF),
             pltpu.VMEM((128, LEN), BF),
             pltpu.VMEM((2, 4, LEN, 256), F32),
+            pltpu.VMEM((4, LEN, 256), BF),
+            pltpu.VMEM((2, 4, 8, 256), F32),
             pltpu.VMEM((LEN, 128), F32),
             pltpu.VMEM((LEN, 128), F32),
             pltpu.VMEM((HD, 4, 32, 1280), BF),
@@ -609,6 +628,8 @@
             pltpu.SMEM((8, 32, 128), jnp.int32),
             pltpu.SMEM((8, 128), jnp.int32),
             sems(2),
+            pltpu.VMEM((HD, 128, OUTW), BF),
+            sems(HD),
         ],
         compiler_params=pltpu.CompilerParams(
             collective_id=0, has_side_effects=True, vmem_limit_bytes=56 * 1024 * 1024
@@ -616,10 +637,43 @@
     )(q, k, v, cot, w, tile_list, owners, *states)
 
 
+def copy_kernel(*refs):
+    sources, targets, held, sem = refs[:8], refs[8:16], refs[16:24], refs[24]
+    pairs = []
+    for source, buffer, target in zip(sources, held, targets):
+        half = source.shape[0] // 2
+        for part in (pl.ds(0, half), pl.ds(half, source.shape[0] - half)):
+            i = len(pairs)
+            pairs.append((
+                pltpu.make_async_copy(source.at[part], buffer.at[part], sem.at[0, i]),
+                pltpu.make_async_copy(buffer.at[part], target.at[part], sem.at[1, i]),
+            ))
+    for load, _ in pairs:
+        load.start()
+    for load, store in pairs:
+        load.wait()
+        store.start()
+    for _, store in pairs:
+        store.wait()
+
+
+def copy_out(*arrays):
+    space = pl.BlockSpec(memory_space=pltpu.MemorySpace.HBM)
+    return pl.pallas_call(
+        copy_kernel,
+        out_shape=[jax.ShapeDtypeStruct(a.shape, a.dtype) for a in arrays],
+        in_specs=[space] * 8,
+        out_specs=[space] * 8,
+        scratch_shapes=[pltpu.VMEM(a.shape, a.dtype) for a in arrays] + [pltpu.SemaphoreType.DMA((2, 16))],
+        compiler_params=pltpu.CompilerParams(vmem_limit_bytes=60 * 1024 * 1024),
+    )(*arrays)
+
+
 def local(q, k, v, cot, w, tile_list, owners, master, one, two, mean):
-    dq, dk, dv, new_w, *states = step(
+    results = step(
         q, k, v, cot, w, tile_list, owners[:, 0], master[0], one[0], two[0], mean[0]
     )
+    dq, dk, dv, new_w, *states = copy_out(*results)
     return (dq, dk, dv, new_w.reshape(HD * 128, OUTW), *[s[None] for s in states])
 
 

time: 171 us -> 161 us (0.942)
  local copies, waits for them, and re-layouts: 10.3 us -> 0 us
    unnamed x22 -> x0, local copies, waits for them, and re-layouts: 10.3 us -> none
    pallas_call x1, Pallas kernels: 160 us -> 153 us  [step(): pl.pallas_call(step_kernel, out_shape=[jax.ShapeDtypeStruct((TOK, OUTW),...]
    pallas_call x0 -> x1, Pallas kernels: none -> 6.69 us  [copy_out(): pl.pallas_call(copy_kernel, out_shape=[jax.ShapeDtypeStruct(a.shape, a.dt...]
where the time goes in v4:
time: 161 us
  Pallas kernels  160 us (99%)
    pallas_call x1, Pallas kernels, step(): pl.pallas_call(step_kernel, out_shape=[jax.ShapeDtypeStruct((TOK, OUTW),...  153 us
    pallas_call x1, Pallas kernels, copy_out(): pl.pallas_call(copy_kernel, out_shape=[jax.ShapeDtypeStruct(a.shape, a.dt...  6.69 us

profile of v4, /device:TPU:0, one launch (start us, length us, event | category | flops | bytes accessed | tf_op | source)
XLA Modules:
  0.0 160.6 jit_solution(16469625983321000213)
XLA Ops:
  0.6 153.1 %shard_map.170 = (bf16[256,2560]{1,0:T(8,128)(2,1)}, bf16[256,2560]{1,0:T(8,128)(2,1)}, bf16[256,2560]{1,0:T(8,128)(2,1)}, bf16[5,128,2560]{2,1,0:T(8,128)(2,1)}...) custom-call(bf16[256,2560]{1,0:T(8,128)(2,1)} %q_in.1, ...), custom_call_target="tpu_custom_call" | custom-call | tf_op jit(solution)/shard_map/pallas_call | solution.py:574
  153.7 6.7 %shard_map.171 = (bf16[256,2560]{1,0:T(8,128)(2,1)}, bf16[256,2560]{1,0:T(8,128)(2,1)}, bf16[256,2560]{1,0:T(8,128)(2,1)}, bf16[5,128,2560]{2,1,0:T(8,128)(2,1)}...) custom-call(bf16[256,2560]{1,0:T(8,128)(2,1)} %get-tuple-element.24.refs_0_,, ...), custom_call_target="tpu_custom_call" | custom-call | tf_op jit(solution)/shard_map/pallas_call | solution.py:662

commit v5 on v4

--- a/solution.py
+++ b/solution.py
@@ -28,7 +28,7 @@
 NEG = -1e30
 SCALE = 1.0 / math.sqrt(128.0)
 SCALE2 = SCALE * math.log2(math.e)
-BACK_ONE, BACK_TWO = 6, 8
+BACK_ONE, BACK_TWO, BACK_THREE = 4, 5, 7
 CC = 4
 
 
@@ -375,6 +375,7 @@
             after_second(h - 1)
 
     after_first(HD - 1)
+    back_start(BACK_ONE, BACK_TWO)
     after_second(HD - 1)
 
     def pack(device):
@@ -386,12 +387,13 @@
         device = lax.rem(dp + k, 32)
         return remote(tx.at[device], rx.at[dp], t_send.at[k - 1], t_recv.at[k - 1], (device, me))
 
-    @pl.loop(1, 32)
-    def _(k):
+    @pl.loop(0, 31)
+    def _(i):
+        k = jnp.where(i < 16, 2 * i + 1, 2 * i - 30)
         pack(lax.rem(dp + k, 32))
         to_owner(k).start()
 
-    back_start(BACK_ONE, BACK_TWO)
+    back_start(BACK_TWO, BACK_THREE)
     backward(HD - 1)
     pack(dp)
     rx[dp] = tx[dp]
@@ -429,11 +431,11 @@
         device = lax.rem(dp + k, 32)
         return remote(pieces.at[device // 2], landed.at[dp], n_send.at[k - 1], n_recv.at[k - 1], (device, me))
 
-    @pl.loop(1, 32)
-    def _(k):
-        from_owner(k).start()
-
-    back_start(BACK_TWO, 3 * HD)
+    @pl.loop(0, 31)
+    def _(i):
+        from_owner(jnp.where(i < 16, 2 * i + 1, 2 * i - 30)).start()
+
+    back_start(BACK_THREE, 3 * HD)
     for i in range(4):
         state_out(i).start()
     landed[dp] = pieces[mine]
@@ -512,23 +514,37 @@
         for f, d in both:
             landed_two(f, i, d, 0).wait_recv()
             ring_two(f, i, d, 1).start()
-    for i in range(4):
-        for f, d in both:
-            landed_two(f, i, d, 1).wait_recv()
 
     def w_copy(h):
         return pltpu.make_async_copy(w_new.at[h], w_out.at[h], w_sem.at[h])
 
-    @pl.loop(0, HD)
-    def _(h):
-        for c in range(10):
-            for j in range(8):
-                low = w16[j // 2, 2 * (j % 2), h * 10 + c].astype(F32)
-                high = w16[j // 2, 2 * (j % 2) + 1, h * 10 + c].astype(F32)
+    def rows_of(first, pairs):
+        for pair in pairs:
+            h, c = pair // 10, pair % 10
+            for m in range(2):
+                low = w16[first, 2 * m, pair].astype(F32)
+                high = w16[first, 2 * m + 1, pair].astype(F32)
+                place = pl.ds(pl.multiple_of(first * 32 + m * 16, 16), 16)
                 left = jnp.concatenate([low[:8], high[:8]], axis=0)
                 right = jnp.concatenate([low[8:], high[8:]], axis=0)
-                w_new[h, j * 16 : (j + 1) * 16, c * 256 : c * 256 + 128] = left.astype(BF)
-                w_new[h, j * 16 : (j + 1) * 16, c * 256 + 128 : c * 256 + 256] = right.astype(BF)
+                w_new[h, place, c * 256 : c * 256 + 128] = left.astype(BF)
+                w_new[h, place, c * 256 + 128 : c * 256 + 256] = right.astype(BF)
+
+    for i in (0, 3, 1, 2):
+        for d in range(2):
+            landed_two(0, i, d, 1).wait_recv()
+        rows_of(ring(x, i), range(25))
+    for h in range(2):
+        w_copy(h).start()
+    for i in range(4):
+        for d in range(2):
+            landed_two(1, i, d, 1).wait_recv()
+
+    @pl.loop(0, 4)
+    def _(first):
+        rows_of(first, range(25, 50))
+
+    for h in range(2, HD):
         w_copy(h).start()
 
     for c in range(CC):

time: 161 us -> 158 us (0.981)
  Pallas kernels: 160 us -> 157 us
    pallas_call x1, Pallas kernels: 153 us -> 150 us  [step(): pl.pallas_call(step_kernel, out_shape=[jax.ShapeDtypeStruct((TOK, OUTW),...]
where the time goes in v5:
time: 158 us; the launch traced here: 157 us
  Pallas kernels  157 us (99%)
    pallas_call x1, Pallas kernels, step(): pl.pallas_call(step_kernel, out_shape=[jax.ShapeDtypeStruct((TOK, OUTW),...  150 us
    pallas_call x1, Pallas kernels, copy_out(): pl.pallas_call(copy_kernel, out_shape=[jax.ShapeDtypeStruct(a.shape, a.dt...  6.69 us

profile of v5, /device:TPU:0, one launch (start us, length us, event | category | flops | bytes accessed | tf_op | source)
XLA Modules:
  0.0 157.4 jit_solution(17771732813409935092)
XLA Ops:
  0.6 149.9 %shard_map.170 = (bf16[256,2560]{1,0:T(8,128)(2,1)}, bf16[256,2560]{1,0:T(8,128)(2,1)}, bf16[256,2560]{1,0:T(8,128)(2,1)}, bf16[5,128,2560]{2,1,0:T(8,128)(2,1)}...) custom-call(bf16[256,2560]{1,0:T(8,128)(2,1)} %q_in.1, ...), custom_call_target="tpu_custom_call" | custom-call | tf_op jit(solution)/shard_map/pallas_call | solution.py:590
  150.6 6.7 %shard_map.171 = (bf16[256,2560]{1,0:T(8,128)(2,1)}, bf16[256,2560]{1,0:T(8,128)(2,1)}, bf16[256,2560]{1,0:T(8,128)(2,1)}, bf16[5,128,2560]{2,1,0:T(8,128)(2,1)}...) custom-call(bf16[256,2560]{1,0:T(8,128)(2,1)} %get-tuple-element.24.refs_0_,, ...), custom_call_target="tpu_custom_call" | custom-call | tf_op jit(solution)/shard_map/pallas_call | solution.py:678

commit v6 on v5

--- a/solution.py
+++ b/solution.py
@@ -86,7 +86,7 @@
     state, tx, rx, pieces, landed, w16,
     state_sem, state_out_sem, t_send, t_recv, n_send, n_recv,
     a_send, a_recv, b_send, b_recv,
-    bias, slot_table, block_table, slot_from, block_from, table_sem, w_new, w_sem,
+    bias, slot_table, block_table, slot_from, block_from, table_sem, w_new, w_sem, half_sum, half_out, half_in, y_send, y_recv,
     ) = refs
     dp, me, x, z, yh = place_of()
     sibling = me + 1 - 2 * lax.rem(me, 2)
@@ -313,6 +313,9 @@
         t = ring(x, p + 1)
         return remote(s2z.at[h, t], r2z.at[h, p], z2_send.at[h, p], z2_recv.at[h, p], (dp_index(t, z, yh), me))
 
+    def other_half(h):
+        return remote(half_out.at[h], half_in.at[h], y_send.at[h], y_recv.at[h], (dp_index(x, z, 1 - yh), me))
+
     def after_first(h):
         for p in range(3):
             first_x(h, p).wait_recv()
@@ -343,6 +346,14 @@
             even = even + r2x[h, p].astype(F32)
             odd = odd + r2z[h, p].astype(F32)
         for i, total in enumerate((even, odd)):
+            half_sum[h, i] = total
+            half_out[h, i] = total.astype(BF)
+        other_half(h).start()
+
+    def after_third(h):
+        other_half(h).wait_recv()
+        for i in range(2):
+            total = half_sum[h, i] + half_in[h, i].astype(F32)
             for u in range(2):
                 for c in range(5):
                     sums[h * 20 + i * 10 + u * 5 + c] = total[u * 8 : u * 8 + 8, c * 128 : c * 128 + 128]
@@ -378,6 +389,10 @@
     back_start(BACK_ONE, BACK_TWO)
     after_second(HD - 1)
 
+    @pl.loop(0, HD)
+    def _(h):
+        after_third(h)
+
     def pack(device):
         tiles = [sums[jnp.clip(slot_from[s, device, 0], 0, HD * 20 - 1)] for s in range(SL)]
         for t in range(4):
@@ -385,33 +400,32 @@
 
     def to_owner(k):
         device = lax.rem(dp + k, 32)
-        return remote(tx.at[device], rx.at[dp], t_send.at[k - 1], t_recv.at[k - 1], (device, me))
-
-    @pl.loop(0, 31)
+        return remote(tx.at[device], rx.at[dp // 2], t_send.at[k // 2 - 1], t_recv.at[k // 2 - 1], (device, me))
+
+    @pl.loop(1, 16)
     def _(i):
-        k = jnp.where(i < 16, 2 * i + 1, 2 * i - 30)
-        pack(lax.rem(dp + k, 32))
-        to_owner(k).start()
+        pack(lax.rem(dp + 2 * i, 32))
+        to_owner(2 * i).start()
 
     back_start(BACK_TWO, BACK_THREE)
     backward(HD - 1)
     pack(dp)
-    rx[dp] = tx[dp]
+    rx[dp // 2] = tx[dp]
     for i in range(4):
         state_copy(i).wait()
 
-    @pl.loop(1, 32)
-    def _(k):
-        to_owner(k).wait_recv()
+    @pl.loop(1, 16)
+    def _(i):
+        to_owner(2 * i).wait_recv()
 
     def state_out(i):
         return pltpu.make_async_copy(state.at[i], states_out[i], state_out_sem.at[i])
 
-    arrived = rx[...].reshape(16, 2, 4, 16, 128)
+    arrived = rx[...]
     even = None
     for s in range(SL):
         if s % 2 == 0:
-            both = arrived[:, 0, s // 2].astype(F32) + arrived[:, 1, s // 2].astype(F32)
+            both = arrived[:, s // 2].astype(F32)
         half = both[:, :8] if s % 2 == 0 else both[:, 8:]
         gradient = half.reshape(128, 128) * (1.0 / 32.0)
         before = [state[i, s] for i in range(4)]
@@ -574,8 +588,15 @@
 
     @pl.loop(1, 32)
     def _(k):
-        to_owner(k).wait_send()
         from_owner(k).wait_send()
+
+    @pl.loop(1, 16)
+    def _(i):
+        to_owner(2 * i).wait_send()
+
+    @pl.loop(0, HD)
+    def _(h):
+        other_half(h).wait_send()
 
     for i in range(4):
         state_out(i).wait()
@@ -624,14 +645,14 @@
             *([sems(HD, 3)] * 8),
             pltpu.VMEM((4, SL, 128, 128), F32),
             pltpu.VMEM((32, 4, 16, 128), BF),
-            pltpu.VMEM((32, 4, 16, 128), BF),
+            pltpu.VMEM((16, 4, 16, 128), BF),
             pltpu.VMEM((16, 4, 16, 128), BF),
             pltpu.VMEM((32, 4, 16, 128), BF),
             pltpu.VMEM((4, 4, 50, 16, 128), BF),
             sems(4),
             sems(4),
-            sems(31),
-            sems(31),
+            sems(15),
+            sems(15),
             sems(31),
             sems(31),
             sems(2, 2, 2),
@@ -645,6 +666,11 @@
             pltpu.SMEM((8, 128), jnp.int32),
             sems(2),
             pltpu.VMEM((HD, 128, OUTW), BF),
+            sems(HD),
+            pltpu.VMEM((HD, 2, 16, 640), F32),
+            pltpu.VMEM((HD, 2, 16, 640), BF),
+            pltpu.VMEM((HD, 2, 16, 640), BF),
+            sems(HD),
             sems(HD),
         ],
         compiler_params=pltpu.CompilerParams(

time: 158 us -> 157 us (level)
  no operation moved by 1% of the time
where the time goes in v6:
time: 157 us; the launch traced here: 156 us
  Pallas kernels  156 us (99%)
    pallas_call x1, Pallas kernels, step(): pl.pallas_call(step_kernel, out_shape=[jax.ShapeDtypeStruct((TOK, OUTW),...  149 us
    pallas_call x1, Pallas kernels, copy_out(): pl.pallas_call(copy_kernel, out_shape=[jax.ShapeDtypeStruct(a.shape, a.dt...  6.69 us

profile of v6, /device:TPU:0, one launch (start us, length us, event | category | flops | bytes accessed | tf_op | source)
XLA Modules:
  0.0 156.4 jit_solution(11560193096987768440)
XLA Ops:
  0.6 148.9 %shard_map.170 = (bf16[256,2560]{1,0:T(8,128)(2,1)}, bf16[256,2560]{1,0:T(8,128)(2,1)}, bf16[256,2560]{1,0:T(8,128)(2,1)}, bf16[5,128,2560]{2,1,0:T(8,128)(2,1)}...) custom-call(bf16[256,2560]{1,0:T(8,128)(2,1)} %q_in.1, ...), custom_call_target="tpu_custom_call" | custom-call | tf_op jit(solution)/shard_map/pallas_call | solution.py:611
  149.5 6.7 %shard_map.171 = (bf16[256,2560]{1,0:T(8,128)(2,1)}, bf16[256,2560]{1,0:T(8,128)(2,1)}, bf16[256,2560]{1,0:T(8,128)(2,1)}, bf16[5,128,2560]{2,1,0:T(8,128)(2,1)}...) custom-call(bf16[256,2560]{1,0:T(8,128)(2,1)} %get-tuple-element.24.refs_0_,, ...), custom_call_target="tpu_custom_call" | custom-call | tf_op jit(solution)/shard_map/pallas_call | solution.py:704
